TPU v7x, 256 devices: a whole 4x4x8 slice. The times are simulated.
256 devices in a mesh: row: 8 (over z_lo, y), col: 32 (over x, z_hi, core).
Axes of the slice: x: 4, y: 4, z: 8 (z_hi: 4, z_lo: 2; z = z_hi * 2 + z_lo), core: 2. Of those that a mesh axis runs over, the one named last changes fastest.
Arguments:
- pair_map: bfloat16 [512, 512, 128], P('row', 'col'), may hold values from -6 to 6
- res_mask: int32 [512], replicated, may hold values from 0 to 1, as said below
- tri_proj: bfloat16 [128, 512], replicated, may hold values from -0.5 to 0.5
- tri_gate: bfloat16 [128, 128], replicated, may hold values from -0.5 to 0.5
- tri_out: bfloat16 [128, 128], replicated, may hold values from -0.5 to 0.5
- att_qkvg: bfloat16 [128, 512], replicated, may hold values from -8 to 8
- att_bias: bfloat16 [128, 4], replicated, may hold values from -1 to 1
- att_out: bfloat16 [128, 128], replicated, may hold values from -0.5 to 0.5
Outputs:
- result: bfloat16 [512, 512, 128], P('row', 'col')
Inputs may be any that keep to these rules, and one draw needn't show every extreme that they name: `res_mask`: the first entry is 1 and the last entry is 0.
All inputs are finite; a program needn't handle non-finite values.
Results may differ from a plain program's by a relative error of at most 0.015.
The roundings to bfloat16 on the way count: a program that leaves them out, or rounds other values in their place, can miss the bound.
Values may be sent and summed in bfloat16 or wider, within the bound.
A program may use at most 256 MiB of HBM per device.

v0:
```python
import math

import jax
import jax.numpy as jnp
from jax import lax
from jax.sharding import PartitionSpec as P

EPS = 1e-05


def from_root(value, axis, root):
    mine = lax.axis_index(axis) == root
    return lax.psum(jnp.where(mine, value, jnp.zeros_like(value)), axis)


def layer_norm(values):
    centre = values - jnp.mean(values, axis=-1, keepdims=True)
    spread = jnp.mean(centre * centre, axis=-1, keepdims=True)
    return centre * lax.rsqrt(spread + EPS)


def local(pair_map, res_mask, tri_proj, tri_gate, tri_out, att_qkvg, att_bias, att_out):
    tile_rows = pair_map.shape[0]
    tile_cols = pair_map.shape[1]
    col_count = lax.axis_size("col")
    residues = tile_cols * col_count
    row_index = lax.axis_index("row")
    col_index = lax.axis_index("col")
    mask_float = res_mask.astype(jnp.float32)
    row_live = lax.dynamic_slice_in_dim(mask_float, row_index * tile_rows, tile_rows)
    col_live = lax.dynamic_slice_in_dim(mask_float, col_index * tile_cols, tile_cols)
    hidden = tri_proj.shape[1] // 4
    normed = layer_norm(pair_map.astype(jnp.float32)).astype(jnp.bfloat16)
    root_index = col_index * tile_cols // tile_rows
    offset = jnp.clip(col_index * tile_cols - row_index * tile_rows, 0, tile_rows - tile_cols)
    projected = jnp.dot(normed, tri_proj, preferred_element_type=jnp.float32)
    sides = jnp.concatenate(
        [
            jax.nn.sigmoid(projected[..., :hidden]) * projected[..., hidden : 2 * hidden],
            jax.nn.sigmoid(projected[..., 2 * hidden : 3 * hidden]) * projected[..., 3 * hidden :],
        ],
        axis=-1,
    )
    both_rows = lax.all_gather(
        (sides * (row_live[:, None, None] * col_live[None, :, None])).astype(jnp.bfloat16),
        "col",
        axis=1,
        tiled=True,
    )
    left_rows = both_rows[..., :hidden]
    own_rows = lax.dynamic_slice_in_dim(both_rows, offset, tile_cols, 0)[..., hidden:]
    right_panel = from_root(own_rows, "row", root_index)
    tri_sum = lax.dot_general(
        left_rows, right_panel, (((1,), (1,)), ((2,), (2,))), preferred_element_type=jnp.float32
    )
    tri_sum = jnp.transpose(tri_sum, (1, 2, 0))
    tri_norm = layer_norm(tri_sum).astype(jnp.bfloat16)
    gating = jax.nn.sigmoid(jnp.dot(normed, tri_gate, preferred_element_type=jnp.float32))
    updated = pair_map.astype(jnp.float32) + gating * jnp.dot(
        tri_norm, tri_out, preferred_element_type=jnp.float32
    )
    normed_two = layer_norm(updated).astype(jnp.bfloat16)
    head_count = att_bias.shape[1]
    head_width = att_qkvg.shape[1] // 4
    head_size = head_width // head_count
    query = jnp.dot(
        normed_two, att_qkvg[:, :head_width], preferred_element_type=jnp.float32
    ).astype(jnp.bfloat16)
    att_gating = jax.nn.sigmoid(
        jnp.dot(normed_two, att_qkvg[:, 3 * head_width :], preferred_element_type=jnp.float32)
    )
    local_pairs = jnp.dot(
        normed_two, att_qkvg[:, head_width : 3 * head_width], preferred_element_type=jnp.float32
    ).astype(jnp.bfloat16)
    local_bias = jnp.dot(normed_two, att_bias, preferred_element_type=jnp.float32).astype(
        jnp.bfloat16
    )
    pair_rows, bias_rows = (
        lax.all_gather(local_pairs, "col", axis=1, tiled=True),
        lax.all_gather(local_bias, "col", axis=1, tiled=True),
    )
    own_bias = lax.dynamic_slice_in_dim(bias_rows, offset, tile_cols, 0)
    bias_panel = from_root(own_bias, "row", root_index)
    bias_heads = jnp.transpose(bias_panel.astype(jnp.float32), (2, 0, 1))
    query_heads = query.reshape(tile_rows, tile_cols, head_count, head_size)
    key_heads = pair_rows[..., :head_width].reshape(tile_rows, residues, head_count, head_size)
    value_heads = pair_rows[..., head_width:].reshape(tile_rows, residues, head_count, head_size)
    scores = jnp.einsum(
        "ijhd,ikhd->ihjk", query_heads, key_heads, preferred_element_type=jnp.float32
    ) / math.sqrt(head_size)
    scores = scores + bias_heads[None]
    scores = jnp.where(mask_float[None, None, None, :] > 0, scores, -1000000000.0)
    scores = scores - jnp.max(scores, axis=-1, keepdims=True)
    exps = jnp.exp(scores)
    weights = (exps / jnp.sum(exps, axis=-1, keepdims=True)).astype(jnp.bfloat16)
    attended = jnp.einsum(
        "ihjk,ikhd->ijhd", weights, value_heads, preferred_element_type=jnp.float32
    )
    attended = attended.reshape(tile_rows, tile_cols, head_width)
    gated = (att_gating * attended).astype(jnp.bfloat16)
    return (updated + jnp.dot(gated, att_out, preferred_element_type=jnp.float32)).astype(
        jnp.bfloat16
    )


def solution(mesh):
    in_specs = (P("row", "col", None), P(), P(), P(), P(), P(), P(), P())
    out_specs = P("row", "col", None)
    return jax.shard_map(local, mesh=mesh, in_specs=in_specs, out_specs=out_specs, check_vma=False)
```

profile of v0, /device:TPU:3, one launch (start us, length us, event | category | flops | bytes accessed | tf_op | source)
XLA Modules:
  0.0 560.2 jit_solution(6150937704540444548)
XLA Ops:
  6.6 1.2 convert_reduce_fusion
  7.8 0.1 copy.62
  7.9 1.3 fusion.21
  9.3 0.1 copy.64
  9.4 1.4 fusion.30
  10.9 0.3 slice_multiply_fusion.1
  11.2 0.7 convert_element_type.40
  11.8 0.1 dynamic_slice.13
  11.9 0.1 dynamic_slice.12
  12.0 0.1 broadcast_multiply_fusion
  12.1 1.0 fusion.18
  13.2 131.3 %all-gather.3.cloned.1.call-done = bf16[64,512,256]{2,1,0:T(8,128)(2,1)} async-done(((bf16[64,16,256]{2,1,0:T(8,128)(2,1)}), bf16[64,512,256]{2,1,0:T(8,128)(2,1)}) %all-gather.3.cloned.1.call-update) | async-done | bytes 16777232 | tf_op jit(solution)/shard_map/all_gather | solution.py:44
  144.5 3.4 dynamic-slice_select_fusion
  148.0 0.7 fusion.13
  148.7 7.6 %slice.48 = bf16[64,512,128]{2,1,0:T(8,128)(2,1)} slice(bf16[64,512,256]{2,1,0:T(8,128)(2,1)} %all-gather.3.cloned.1.call-done), slice={[0:64], [0:512], [0:128]} | slice | bytes 16777216 | tf_op jit(solution)/shard_map/slice | solution.py:50
  156.3 12.6 %copy.65 = bf16[64,512,128]{1,0,2:T(8,128)(2,1)} copy(bf16[64,512,128]{2,1,0:T(8,128)(2,1)} %slice.48) | data formatting | bytes 16777216 | tf_op jit(solution)/shard_map/slice | solution.py:50
  168.9 61.3 %all-reduce.3.cloned.1.call-done = bf16[16,512,128]{2,1,0:T(8,128)(2,1)} async-done(((bf16[16,512,128]{2,1,0:T(8,128)(2,1)}), bf16[16,512,128]{2,1,0:T(8,128)(2,1)}) %all-reduce.3.cloned.1.call-update) | async-done | bytes 2097168 | tf_op jit(solution)/shard_map/psum | solution.py:13
  230.2 3.4 copy.66
  233.7 5.7 %fusion.50 = (f32[64,16]{0,1:T(8,128)S(1)}, f32[64,16,128]{0,1,2:T(8,128)S(1)}) fusion(bf16[64,512,128]{1,0,2:T(8,128)(2,1)} %copy.65, bf16[16,512,128]{1,0,2:T(8,128)(2,1)S(1)} %copy.66), kind=kOutput, calls=%fused_computation.79 | convolution fusion | flops 134347776 | bytes 11014144 | tf_op jit(solution)/shard_map/dot_general | solution.py:53
  239.4 0.2 multiply_reduce_fusion
  239.6 0.1 multiply_convert_fusion
  239.7 0.6 copy.67
  240.3 0.4 fusion.51
  240.8 0.1 copy.69
  240.9 0.4 multiply_reduce_fusion.1
  241.3 0.1 copy.71
  241.4 0.8 convolution_convert_fusion.2
  242.2 0.1 copy.76
  242.3 44.5 %all_gather.11 = bf16[64,512,4]{0,2,1:T(4,128)(2,1)S(1)} all-gather(bf16[64,16,4]{0,2,1:T(4,128)(2,1)S(1)} %copy.76), channel_id=1, replica_groups=mesh['row'=8,'col'=32] {'col'}, dimensions={1}, use_global_device_ids=true | all-gather | bytes 270336 | tf_op jit(solution)/shard_map/all_gather | solution.py:80
  286.8 0.3 constant_dynamic-slice_fusion
  287.1 0.3 copy.80
  287.4 0.7 select_bitcast_fusion
  288.1 0.2 all-gather.5.cloned.1.call-start
  288.3 1.3 convolution_convert_fusion
  289.6 0.4 convolution_convert_fusion.1
  290.1 0.3 copy.73
  290.4 1.6 copy.75
  292.0 67.8 %all-reduce.5.cloned.1.call-done = bf16[4,16,512]{2,1,0:T(8,128)(2,1)} async-done(((bf16[4,16,512]{2,1,0:T(8,128)(2,1)}), bf16[4,16,512]{2,1,0:T(8,128)(2,1)}) %all-reduce.5.cloned.1.call-update) | async-done | bytes 65552 | tf_op jit(solution)/shard_map/psum | solution.py:13
  359.8 0.8 transpose.28
  360.6 134.4 %all-gather.5.cloned.1.call-done = bf16[64,512,256]{2,1,0:T(8,128)(2,1)} async-done(((bf16[64,16,256]{2,1,0:T(8,128)(2,1)}), bf16[64,512,256]{2,1,0:T(8,128)(2,1)}) %all-gather.5.cloned.1.call-update) | async-done | bytes 16777232 | tf_op jit(solution)/shard_map/all_gather | solution.py:79
  495.0 11.6 %fusion.49 = (bf16[64,512,128]{2,1,0:T(8,128)(2,1)}, bf16[64,512,128]{2,1,0:T(8,128)(2,1)}) fusion(bf16[64,512,256]{2,1,0:T(8,128)(2,1)} %all-gather.5.cloned.1.call-done), kind=kLoop, calls=%fused_computation.78 | loop fusion | bytes 33554432 | tf_op jit(solution)/shard_map/slice | solution.py:86
  506.6 11.9 %copy.72 = bf16[64,512,128]{1,2,0:T(8,128)(2,1)} copy(bf16[64,512,128]{2,1,0:T(8,128)(2,1)} %get-tuple-element.6) | data formatting | bytes 16777216 | tf_op jit(solution)/shard_map/slice | solution.py:87
  518.5 11.9 %copy.74 = bf16[64,512,128]{1,2,0:T(8,128)(2,1)} copy(bf16[64,512,128]{2,1,0:T(8,128)(2,1)} %get-tuple-element.5) | data formatting | bytes 16777216 | tf_op jit(solution)/shard_map/slice | solution.py:86
  530.4 9.3 %fusion.52 = (f32[64,4,16]{2,1,0:T(4,128)S(1)}, f32[64,4,16,512]{3,2,1,0:T(8,128)}) fusion(f32[4,16,512]{2,1,0:T(8,128)S(1)} %transpose.28, pred[512]{0:T(512)(128)(4,1)S(1)} %broadcast_compare_fusion, bf16[64,16,4,32]{3,1,2,0:T(8,128)(2,1)S(1)} %copy.75, bf16[64,512,4,32]{1,3,2,0:T(8,128)(2,1)} %bitcast.46), kind=kOutput, calls=%fused_computation.81 | convolution fusion | flops 144704000 | bytes 17187328 | tf_op jit(solution)/shard_map/sub | solution.py:93
  539.7 9.5 %fusion.7 = f32[64,16,4,32]{3,1,2,0:T(8,128)} fusion(bf16[64,512,4,32]{1,3,2,0:T(8,128)(2,1)} %bitcast.45, f32[64,4,16,512]{3,2,1,0:T(8,128)} %get-tuple-element.14, f32[64,4,16]{2,1,0:T(4,128)S(1)} %get-tuple-element.13), kind=kOutput, calls=%fused_computation.11 | convolution fusion | flops 138412032 | bytes 17317888 | tf_op jit(solution)/shard_map/ihjk,ikhd->ijhd/dot_general | solution.py:96
  549.3 2.7 copy.78
  551.9 0.4 copy.79
  552.3 1.3 fusion.17
  (36 shorter events, 0.5 us)
Async XLA Ops:
  6.5 2.9 copy-start
  6.5 141.4 %copy-start.2 = (bf16[64,16,128]{2,1,0:T(8,128)(2,1)S(1)}, bf16[64,16,128]{2,1,0:T(8,128)(2,1)}, u32[]{:S(2)}) copy-start(bf16[64,16,128]{2,1,0:T(8,128)(2,1)} %param.8) | copy-start | bytes 786436
  6.5 141.4 %copy-start.6 = (bf16[128,128]{1,0:T(8,128)(2,1)S(1)}, bf16[128,128]{1,0:T(8,128)(2,1)}, u32[]{:S(2)}) copy-start(bf16[128,128]{1,0:T(8,128)(2,1)} %param.11) | copy-start | bytes 98308
  6.5 138.0 %all-gather.3.cloned.1.call-start = ((), (), s32[]{:S(2)}) async-start(), calls=%async_computation | async-start | bytes 17301504 | tf_op jit(solution)/shard_map/all_gather | solution.py:44
  13.1 217.1 %all-reduce.3.cloned.1.call-start = ((), (), s32[]{:S(2)}) async-start(), calls=%async_computation.1 | async-start | bytes 4194304 | tf_op jit(solution)/shard_map/psum | solution.py:13
  147.9 211.9 %all-reduce.5.cloned.1.call-start = ((), (), s32[]{:S(2)}) async-start(), calls=%async_computation.3 | async-start | bytes 131072 | tf_op jit(solution)/shard_map/psum | solution.py:13
  233.6 6.7 %copy-start.4 = (bf16[128,128]{1,0:T(8,128)(2,1)S(1)}, bf16[128,128]{1,0:T(8,128)(2,1)}, u32[]{:S(2)}) copy-start(bf16[128,128]{1,0:T(8,128)(2,1)} %param.12) | copy-start | bytes 98308
  233.7 7.7 %copy-start.8 = (bf16[128,4]{0,1:T(4,128)(2,1)S(1)}, bf16[128,4]{0,1:T(4,128)(2,1)}, u32[]{:S(2)}) copy-start(bf16[128,4]{0,1:T(4,128)(2,1)} %param.14) | copy-start | bytes 3076
  233.7 54.6 %copy-start.3 = (bf16[128,512]{1,0:T(8,128)(2,1)S(1)}, bf16[128,512]{1,0:T(8,128)(2,1)}, u32[]{:S(2)}) copy-start(bf16[128,512]{1,0:T(8,128)(2,1)} %param.13) | copy-start | bytes 393220
  239.4 50.2 %copy-start.5 = (s32[512]{0:T(512)S(1)}, s32[512]{0:T(512)}, u32[]{:S(2)}) copy-start(s32[512]{0:T(512)} %param.9) | copy-start | bytes 6148
  288.1 206.9 %all-gather.5.cloned.1.call-start = ((), (), s32[]{:S(2)}) async-start(), calls=%async_computation.2 | async-start | bytes 17301504 | tf_op jit(solution)/shard_map/all_gather | solution.py:79
  539.7 12.6 %copy-start.7 = (bf16[128,128]{1,0:T(8,128)(2,1)S(1)}, bf16[128,128]{1,0:T(8,128)(2,1)}, u32[]{:S(2)}) copy-start(bf16[128,128]{1,0:T(8,128)(2,1)} %param.15) | copy-start | bytes 98308
  539.7 13.9 %copy-start.1 = (bf16[128,512]{1,0:T(8,128)(2,1)S(1)}, bf16[128,512]{1,0:T(8,128)(2,1)}, u32[]{:S(2)}) copy-start(bf16[128,512]{1,0:T(8,128)(2,1)} %param.10) | copy-start | bytes 393220
Sparse Core Ops, SparseCore 0:
  13.2 131.2 all-gather.2
  148.0 82.1 all-reduce.2
  288.2 71.5 all-reduce.4
  362.4 132.5 all-gather.4
where the time goes:
time: 563 us; the launch traced here: 560 us
  waiting for transfers between devices  395 us (70%)
  local copies, waits for them, and re-layouts  66.2 us (12%)
  blocking collectives  44.5 us (8%)
  matrix products  30.8 us (5%)
  between operations  13.4 us (2%)
  other arithmetic  10.2 us (2%)
    all_gather x1, waiting for transfers between devices, local(): lax.all_gather(local_pairs, 'col', axis=1, tiled=True)  134 us
    all_gather x1, waiting for transfers between devices, local(): lax.all_gather((sides * (row_live[:, None, None] * col_live[None, :, None...  131 us
    psum x2, waiting for transfers between devices, from_root(): return lax.psum(jnp.where(mine, value, jnp.zeros_like(value)), axis)  129 us
    all_gather x1, blocking collectives, local(): lax.all_gather(local_bias, 'col', axis=1, tiled=True)  44.5 us
    slice x2, local copies, waits for them, and re-layouts, local(): pair_rows[..., :head_width]  23.5 us
    slice x2, local copies, waits for them, and re-layouts, local(): left_rows = both_rows[..., :hidden]  20.2 us
    slice x1, local copies, waits for them, and re-layouts, local(): pair_rows[..., head_width:]  11.9 us
  transfers between devices with their start and end apart: 4, of which 4 were waited for; matrix products, arithmetic and copies ran while one was open for 5% of the time, Pallas kernels for 0%

commit v1 on v0

v1 whole, which is shorter than its diff:
```python
import math

import jax
import jax.numpy as jnp
from jax import lax
from jax.experimental import pallas as pl
from jax.experimental.pallas import tpu as pltpu
from jax.sharding import PartitionSpec as P

EPS = 1e-05
MESH = pl.DeviceIdType.MESH
F32 = jnp.float32
BF16 = jnp.bfloat16
NT = (((1,), (1,)), ((), ()))


def loop(low, high, body):
    def step(index, carry):
        body(index)
        return carry

    lax.fori_loop(low, high, step, 0)


def norm_over(values, axis):
    centre = values - jnp.mean(values, axis=axis, keepdims=True)
    spread = jnp.mean(centre * centre, axis=axis, keepdims=True)
    return centre * lax.rsqrt(spread + EPS)


def dot(a, b):
    return jnp.dot(a, b, preferred_element_type=F32)


def dot_nt(a, b):
    return lax.dot_general(a, b, NT, preferred_element_type=F32)


def flip(values):
    return values.astype(F32).T.astype(BF16)


def wait_bytes(ref, sem):
    pltpu.make_async_copy(ref, ref, sem).wait()


def kernel(
    pair_ref, mask_smem, mask_ref, proj_ref, gate_ref, tout_ref, qkvg_ref, abias_ref, aout_ref,
    out_ref,
    xf, xn, nk, wpt, ms, sb, pt, gt, gate_t, tout_t, qkvg_t,
    a_buf, rt, s_buf, t_buf, updt, n2s, ns, bscr, bm, up,
    x_buf, bias, kb, vt, qt, gq, gs, h_buf,
    send1, recv1, fsend, frecv, send2, recv2, send3, recv3, bs1, br1, bs2, br2, send4, recv4,
):
    r = lax.axis_index("row")
    c = lax.axis_index("col")
    q = lax.div(c, 2)
    p = lax.rem(c, 2)
    chip = r * 16 + q
    half = lax.div(r, 4)
    rl = lax.rem(r, 4)
    sibling = (r, c + 1 - 2 * p)

    barrier = pltpu.get_barrier_semaphore()

    def greet_same(off):
        d = lax.rem(chip + off, 128)
        pl.semaphore_signal(
            barrier, inc=1, device_id=(lax.div(d, 16), 2 * lax.rem(d, 16) + p), device_id_type=MESH
        )

    def greet_cross(off):
        pl.semaphore_signal(barrier, inc=1, device_id=(r, 2 * off + 1 - p), device_id_type=MESH)

    loop(1, 128, greet_same)
    loop(0, 16, greet_cross)

    lane = lax.broadcasted_iota(jnp.int32, (1, 128), 1)
    low = lane < 64

    def half_lanes(a, b):
        return jnp.where(low, a, b)

    def swap(values):
        return pltpu.roll(values, 64, 1)

    flat = pair_ref[...].astype(F32).reshape(1024, 128)
    xf[...] = flat
    xn[...] = norm_over(flat, 1).astype(BF16).astype(F32)
    wpt[...] = flip(proj_ref[...])
    for k in range(16):
        part = xn[pl.ds(k, 64, stride=16), :].astype(BF16)
        nk[k] = jnp.concatenate([part, part], axis=0)

    two = mask_ref[pl.ds(lax.div(r, 2), 1), :].astype(F32)
    odd = lax.rem(r, 2) == 1
    turned = swap(jnp.broadcast_to(two, (8, 128)))[0:1]
    row_live = half_lanes(jnp.where(odd, turned, two), jnp.where(odd, two, turned))
    col_live = [mask_smem[c * 16 + k].astype(F32) for k in range(16)]

    pl.semaphore_wait(barrier, 143)

    def project(step):
        block = lax.rem(lax.div(r, 2) + step, 4)
        first = pl.multiple_of(block * 32, 32)
        weights = jnp.concatenate([wpt[pl.ds(128 * b + first, 32), :] for b in range(4)], axis=0)
        for k in range(16):
            z = dot_nt(weights, nk[k])
            g = half_lanes(z[0:32], z[64:96])
            v = half_lanes(z[32:64], z[96:128])
            ms[pl.ds(k, 32, stride=16), :] = jax.nn.sigmoid(g) * v * (row_live * col_live[k])
        sb[pl.ds(first, 32)] = ms[...].astype(BF16).reshape(32, 16, 128)

        def send(off):
            ch = first + lax.rem(chip + off, 32)
            pltpu.make_async_remote_copy(
                src_ref=sb.at[ch],
                dst_ref=a_buf.at[p, r, q],
                send_sem=send1,
                recv_sem=recv1.at[r],
                device_id=(lax.div(ch, 16), 2 * lax.rem(ch, 16) + p),
                device_id_type=MESH,
            ).start()

        @pl.when(step == 0)
        def _():
            pltpu.make_async_copy(sb.at[chip], a_buf.at[p, r, q], recv1.at[r]).start()

        loop(jnp.where(step == 0, 1, 0), 32, send)

    loop(0, 4, project)

    gate_t[...] = flip(gate_ref[...])
    tout_t[...] = flip(tout_ref[...])
    qkvg_t[...] = flip(qkvg_ref[...])

    def prepare(s):
        pos = jnp.concatenate(
            [xf[pl.ds(s, 64, stride=16), :], xf[pl.ds(s + 8, 64, stride=16), :]], axis=0
        )
        pt[s] = pos.T
        norm_pos = jnp.concatenate([nk[s, 0:64], nk[s + 8, 0:64]], axis=0)
        gt[s] = jax.nn.sigmoid(dot_nt(gate_t[...], norm_pos))

    loop(0, 8, prepare)

    def forward_copy(row):
        return pltpu.make_async_remote_copy(
            src_ref=a_buf.at[p, row],
            dst_ref=a_buf.at[p, row],
            send_sem=fsend.at[row],
            recv_sem=frecv.at[row],
            device_id=sibling,
            device_id_type=MESH,
        )

    def forward(step):
        row = lax.rem(r + step, 8)
        wait_bytes(a_buf.at[p, row], recv1.at[row])
        forward_copy(row).start()

    loop(0, 8, forward)

    def turn(row):
        wait_bytes(a_buf.at[1 - p, row], frecv.at[row])
        both = a_buf[:, row].reshape(512, 128)
        both_t = flip(both)
        for cc in range(2):
            rt[pl.ds(pl.multiple_of(row * 32 + cc * 16, 16), 16), :] = jnp.where(
                p == 0, both_t[64 + 32 * cc : 80 + 32 * cc], both_t[80 + 32 * cc : 96 + 32 * cc]
            )

    loop(0, 8, turn)

    def triangle(step):
        row = lax.rem(r + step, 8)
        prod = dot(rt[...], a_buf[:, row].reshape(512, 128)).reshape(16, 2, 8, 128)
        hi = swap(prod[:, 1].reshape(128, 128)).reshape(16, 8, 128)
        s_buf[row] = jnp.where(low[None], prod[:, 0], hi)

        def send(off):
            to = lax.rem(q + off, 16)
            pltpu.make_async_remote_copy(
                src_ref=s_buf.at[row, to],
                dst_ref=t_buf.at[pl.ds(pl.multiple_of(chip * 8, 8), 8), :],
                send_sem=send2,
                recv_sem=recv2,
                device_id=(row, 2 * to + p),
                device_id_type=MESH,
            ).start()

        @pl.when(step == 0)
        def _():
            pltpu.make_async_copy(
                s_buf.at[row, q], t_buf.at[pl.ds(pl.multiple_of(chip * 8, 8), 8), :], recv2
            ).start()

        loop(jnp.where(step == 0, 1, 0), 16, send)

    loop(0, 8, triangle)

    wait_bytes(t_buf, recv2)

    def home(s):
        tri = t_buf[pl.ds(s, 128, stride=8), :]
        tri_norm = norm_over(tri, 0).astype(BF16)
        updated = pt[s] + gt[s] * dot(tout_t[...], tri_norm)
        updt[s] = updated
        norm_two = norm_over(updated, 0)
        here = jnp.where(
            low, mask_smem[c * 16 + s].astype(F32), mask_smem[c * 16 + s + 8].astype(F32)
        )
        heads = dot(abias_ref[...], norm_two.astype(BF16))[0:8]
        bscr[pl.ds(s, 8, stride=8), :] = jnp.where(here > 0, heads, -1000000000.0)
        turned = norm_two.T
        n2s[pl.ds(s, 64, stride=16), :] = turned[0:64]
        n2s[pl.ds(s + 8, 64, stride=16), :] = turned[64:128]

    loop(0, 8, home)

    for pair in range(2):
        h0 = bscr[16 * pair : 16 * pair + 8, :]
        h1 = bscr[16 * pair + 8 : 16 * pair + 16, :]
        tile = jnp.concatenate([half_lanes(h0, swap(h1)), half_lanes(swap(h0), h1)], axis=0)
        bm[:, 128 * pair : 128 * pair + 128] = tile.astype(BF16)

    def bias_copy(to):
        return pltpu.make_async_remote_copy(
            src_ref=bm,
            dst_ref=bias.at[rl, c],
            send_sem=bs1,
            recv_sem=br1,
            device_id=(r, 2 * to + half),
            device_id_type=MESH,
        )

    def bias_send(off):
        bias_copy(lax.rem(q + off, 16)).start()

    @pl.when(p == half)
    def _():
        pltpu.make_async_copy(bm, bias.at[rl, c], br1).start()

    @pl.when(p != half)
    def _():
        bias_copy(q).start()

    loop(1, 16, bias_send)

    ns[...] = n2s[...].astype(BF16).reshape(64, 16, 128)
    pltpu.make_async_copy(ns.at[pl.ds(4 * q, 4)], x_buf.at[:, c], recv3).start()

    def rows_send(off):
        to = lax.rem(c + off, 32)
        pltpu.make_async_remote_copy(
            src_ref=ns.at[pl.ds(4 * lax.div(to, 2), 4)],
            dst_ref=x_buf.at[:, c],
            send_sem=send3,
            recv_sem=recv3,
            device_id=(r, to),
            device_id_type=MESH,
        ).start()

    loop(1, 32, rows_send)

    def bias_row_copy(off):
        return pltpu.make_async_remote_copy(
            src_ref=bias.at[rl],
            dst_ref=bias.at[rl],
            send_sem=bs2.at[off - 1],
            recv_sem=br2.at[rl],
            device_id=(lax.rem(r + off, 8), c),
            device_id_type=MESH,
        )

    @pl.when(p == half)
    def _():
        wait_bytes(bias.at[rl], br1)
        loop(1, 8, lambda off: bias_row_copy(off).start())

    def restore(s):
        turned = updt[s].T
        up[pl.ds(s, 64, stride=16), :] = turned[0:64]
        up[pl.ds(s + 8, 64, stride=16), :] = turned[64:128]

    loop(0, 8, restore)

    wait_bytes(x_buf, recv3)

    def qkvg(i):
        rows = x_buf[i].reshape(512, 128)
        mine = x_buf[i, pl.ds(16 * p, 16)].reshape(256, 128)
        kb[i] = dot(rows, qkvg_ref[:, 128:256]).astype(BF16)
        vt[i] = dot_nt(qkvg_t[256:384, :], rows).astype(BF16)
        qt[i] = dot_nt(qkvg_t[0:128, :], mine).astype(BF16).astype(F32)
        gq[i] = jax.nn.sigmoid(dot_nt(qkvg_t[384:512, :], mine))

    loop(0, 4, qkvg)

    head_of_row = lax.broadcasted_iota(jnp.int32, (128, 128), 0) // 32
    head_of_lane = lax.broadcasted_iota(jnp.int32, (128, 128), 1) // 64
    scale = 1.0 / math.sqrt(32.0)

    def attend(t):
        for e in range(2):
            block = 2 * t + e

            @pl.when(jnp.logical_or(p != half, rl != block))
            def _():
                wait_bytes(bias.at[block], br2.at[block])

        def row(i):
            x = qt[i, :, pl.ds(pl.multiple_of(128 * t, 128), 128)]
            xs = swap(x)
            outs = []
            for e in range(2):
                d = half_lanes(x, xs) if e == 0 else half_lanes(xs, x)
                queries = jnp.concatenate(
                    [jnp.where(head_of_row == head_of_lane + 2 * pair, d, 0.0) for pair in range(2)],
                    axis=1,
                ).astype(BF16)
                scores = dot(kb[i], queries) * scale
                scores = scores + bias[2 * t + e].reshape(512, 256).astype(F32)
                exps = jnp.exp(scores - jnp.max(scores, axis=0, keepdims=True))
                weights = exps * (1.0 / jnp.sum(exps, axis=0, keepdims=True))
                outs.append(dot(vt[i], weights.astype(BF16)))
            parts = []
            for h in range(4):
                at = (h // 2) * 128
                first = outs[0][32 * h : 32 * h + 32, at : at + 128]
                second = outs[1][32 * h : 32 * h + 32, at : at + 128]
                if h % 2 == 0:
                    parts.append(half_lanes(first, swap(second)))
                else:
                    parts.append(half_lanes(swap(first), second))
            attended = jnp.concatenate(parts, axis=0)
            gated = gq[i, :, pl.ds(pl.multiple_of(128 * t, 128), 128)] * attended
            gs[i, pl.ds(8 * t, 8)] = gated.T.astype(BF16).reshape(8, 16, 128)

        loop(0, 4, row)

        def send(off):
            cl = 8 * t + off
            to = 16 * p + cl

            @pl.when(to == c)
            def _():
                pltpu.make_async_copy(gs.at[:, cl], h_buf.at[pl.ds(4 * q, 4)], recv4).start()

            @pl.when(to != c)
            def _():
                pltpu.make_async_remote_copy(
                    src_ref=gs.at[:, cl],
                    dst_ref=h_buf.at[pl.ds(4 * q, 4)],
                    send_sem=send4,
                    recv_sem=recv4,
                    device_id=(r, to),
                    device_id_type=MESH,
                ).start()

        loop(0, 8, send)

    loop(0, 2, attend)

    wait_bytes(sb.at[pl.ds(0, 127)], send1)
    loop(0, 8, lambda row: forward_copy(row).wait_send())
    wait_bytes(t_buf.at[pl.ds(0, 127 * 8), :], send2)
    wait_bytes(x_buf.at[:, pl.ds(0, 31)], send3)
    wait_bytes(bias.at[0, pl.ds(0, 15)], bs1)

    @pl.when(p != half)
    def _():
        wait_bytes(bias.at[0, 0], bs1)

    @pl.when(p == half)
    def _():
        loop(1, 8, lambda off: bias_row_copy(off).wait_send())

    wait_bytes(gs.at[:, pl.ds(0, 15)], send4)

    @pl.when(lax.div(c, 16) != p)
    def _():
        wait_bytes(gs.at[:, 0], send4)

    wait_bytes(h_buf, recv4)
    product = dot(h_buf[...].reshape(1024, 128), aout_ref[...])
    out_ref[...] = (up[...] + product).astype(BF16).reshape(64, 16, 128)


def local(pair_map, res_mask, tri_proj, tri_gate, tri_out, att_qkvg, att_bias, att_out):
    bias_rows = jnp.pad(att_bias.T, ((0, 12), (0, 0)))
    vmem = pl.BlockSpec(memory_space=pltpu.VMEM)
    smem = pl.BlockSpec(memory_space=pltpu.SMEM)
    dma = pltpu.SemaphoreType.DMA
    return pl.pallas_call(
        kernel,
        out_shape=jax.ShapeDtypeStruct((64, 16, 128), BF16),
        in_specs=[vmem, smem, vmem, vmem, vmem, vmem, vmem, vmem, vmem],
        out_specs=vmem,
        scratch_shapes=[
            pltpu.VMEM((1024, 128), F32),
            pltpu.VMEM((1024, 128), F32),
            pltpu.VMEM((16, 128, 128), BF16),
            pltpu.VMEM((512, 128), BF16),
            pltpu.VMEM((512, 128), F32),
            pltpu.VMEM((128, 16, 128), BF16),
            pltpu.VMEM((8, 128, 128), F32),
            pltpu.VMEM((8, 128, 128), F32),
            pltpu.VMEM((128, 128), BF16),
            pltpu.VMEM((128, 128), BF16),
            pltpu.VMEM((512, 128), BF16),
            pltpu.VMEM((2, 8, 16, 16, 128), BF16),
            pltpu.VMEM((256, 512), BF16),
            pltpu.VMEM((8, 16, 8, 128), F32),
            pltpu.VMEM((1024, 128), F32),
            pltpu.VMEM((8, 128, 128), F32),
            pltpu.VMEM((1024, 128), F32),
            pltpu.VMEM((64, 16, 128), BF16),
            pltpu.VMEM((64, 128), F32),
            pltpu.VMEM((16, 256), BF16),
            pltpu.VMEM((1024, 128), F32),
            pltpu.VMEM((4, 32, 16, 128), BF16),
            pltpu.VMEM((4, 32, 16, 256), BF16),
            pltpu.VMEM((4, 512, 128), BF16),
            pltpu.VMEM((4, 128, 512), BF16),
            pltpu.VMEM((4, 128, 256), F32),
            pltpu.VMEM((4, 128, 256), F32),
            pltpu.VMEM((4, 16, 16, 128), BF16),
            pltpu.VMEM((64, 16, 128), BF16),
            dma, dma((8,)),
            dma((8,)), dma((8,)),
            dma, dma,
            dma, dma,
            dma, dma,
            dma((7,)), dma((4,)),
            dma, dma,
        ],
        compiler_params=pltpu.CompilerParams(
            collective_id=0, has_side_effects=True, vmem_limit_bytes=40 * 1024 * 1024
        ),
    )(
        pair_map, res_mask, res_mask.reshape(4, 128), tri_proj, tri_gate, tri_out, att_qkvg,
        bias_rows, att_out,
    )


def solution(mesh):
    in_specs = (P("row", "col", None), P(), P(), P(), P(), P(), P(), P())
    out_specs = P("row", "col", None)
    return jax.shard_map(local, mesh=mesh, in_specs=in_specs, out_specs=out_specs, check_vma=False)
```

time: 563 us -> 106 us (0.19)
  the two profiles are of different devices: /device:TPU:3 before, /device:TPU:59 now
where the time goes in v1:
time: 106 us
  Pallas kernels  99 us (93%)
  local copies, waits for them, and re-layouts  7.09 us (7%)
    pallas_call x1, Pallas kernels, local(): pl.pallas_call(kernel, out_shape=jax.ShapeDtypeStruct((64, 16, 128), BF16...  99 us
    unnamed x17, local copies, waits for them, and re-layouts  7.09 us

profile of v1, /device:TPU:59, one launch (start us, length us, event | category | flops | bytes accessed | tf_op | source)
XLA Modules:
  0.0 106.1 jit_solution(9354065583106046398)
XLA Ops:
  0.0 0.0 copy-start.7
  0.0 0.7 copy-done.7
  0.7 0.0 copy-start.6
  0.7 0.7 copy-done.6
  1.4 0.0 copy-start
  1.4 0.9 copy-done
  2.3 0.0 copy-start.1
  2.3 0.9 copy-done.1
  3.2 0.0 copy-start.2
  3.2 0.9 copy-done.2
  4.1 0.0 copy-start.3
  4.1 0.8 copy-done.3
  4.9 0.0 copy-start.4
  4.9 0.8 copy-done.4
  5.6 0.0 copy-start.5
  5.6 0.8 copy-done.5
  6.4 99.0 %shard_map.82 = bf16[64,16,128]{2,1,0:T(8,128)(2,1)S(1)} custom-call(bf16[64,16,128]{2,1,0:T(8,128)(2,1)S(1)} %copy-done, s32[512]{0:T(512)S(1)} %copy-done.6, s32[4,128]{1,0:T(4,128)S(1)} %bitcast.2, bf16[128,512]{1,0:T(8,128)(2,1)S(1)} %copy-done.1, bf16[128,128]{1,0:T(8,128)(2,1)S(1)} %copy-done.3, bf16[128,128]{1,0:T(8,128)(2,1)S(1)} %copy-done.4, ...), custom_call_target="tpu_custom_call" | custom-call | tf_op jit(solution)/shard_map/pallas_call | solution.py:395
  105.4 0.7 copy.10
  (1 shorter events, 0.0 us)
Async XLA Ops:
  0.0 0.7 copy-start.7
  0.7 0.7 copy-start.6
  1.4 0.9 copy-start
  2.3 0.9 copy-start.1
  3.2 0.9 copy-start.2
  4.1 0.8 copy-start.3
  4.9 0.8 copy-start.4
  5.6 0.8 copy-start.5

commit v2 on v1

v2 whole, which is shorter than its diff:
```python
import math

import jax
import jax.numpy as jnp
from jax import lax
from jax.experimental import pallas as pl
from jax.experimental.pallas import tpu as pltpu
from jax.sharding import PartitionSpec as P

EPS = 1e-05
MESH = pl.DeviceIdType.MESH
F32 = jnp.float32
BF16 = jnp.bfloat16
NT = (((1,), (1,)), ((), ()))
FAR4 = (2, 3, 1, 0)
FAR8 = (4, 5, 7, 3, 6, 2, 1, 0)


def loop(low, high, body, unroll=None):
    def step(index, carry):
        body(index)
        return carry

    lax.fori_loop(low, high, step, 0, unroll=unroll)


def norm_over(values, axis):
    centre = values - jnp.mean(values, axis=axis, keepdims=True)
    spread = jnp.mean(centre * centre, axis=axis, keepdims=True)
    return centre * lax.rsqrt(spread + EPS)


def dot(a, b):
    return jnp.dot(a, b, preferred_element_type=F32)


def dot_nt(a, b):
    return lax.dot_general(a, b, NT, preferred_element_type=F32)


def flip(values):
    return values.astype(F32).T.astype(BF16)


def wait_bytes(ref, sem):
    pltpu.make_async_copy(ref, ref, sem).wait()


def kernel(
    pair_hbm, mask_hbm, mask_rows_hbm, proj_hbm, gate_hbm, tout_hbm, qkvg_hbm, abias_hbm, aout_hbm,
    out_ref,
    pair_ref, mask_smem, mask_ref, proj_ref, gate_ref, tout_ref, qkvg_ref, abias_ref, aout_ref, loads,
    xf, xn, nk, wpt, ms, sb, pt, gt, gate_t, tout_t, qkvg_t,
    a_buf, rt, s_buf, t_buf, tf, updt, n2s, ns, bscr, bm, up,
    x_buf, bias, kb, vt, qt, gq, gs, h_buf,
    send1, recv1, fsend, frecv, send2, recv2, gsend, grecv, send3, recv3, xsend, xrecv,
    bsend, bz, ba, bb, bya, bxb, send4, recv4,
):
    r = lax.axis_index("row")
    c = lax.axis_index("col")
    q = c >> 1
    p = c & 1
    chip = r * 16 + q
    half = r >> 2
    y = r & 3
    x = c >> 3
    zh = q & 3
    sibling = (r, c ^ 1)

    fetches = [
        pltpu.make_async_copy(source, target, loads.at[at])
        for at, (source, target) in enumerate(
            [
                (pair_hbm, pair_ref), (mask_hbm, mask_smem), (mask_rows_hbm, mask_ref),
                (proj_hbm, proj_ref), (gate_hbm, gate_ref), (tout_hbm, tout_ref),
                (qkvg_hbm, qkvg_ref), (abias_hbm, abias_ref), (aout_hbm, aout_ref),
            ]
        )
    ]
    for fetch in fetches:
        fetch.start()

    barrier = pltpu.get_barrier_semaphore()

    def greet(row, col):
        pl.semaphore_signal(barrier, inc=1, device_id=(row, col), device_id_type=MESH)

    for dz in FAR8:
        for dy in FAR4:
            for dx in FAR4:
                if dz or dy or dx:
                    greet(r ^ ((dz & 1) << 2 | dy), c ^ (dx << 3 | (dz >> 1) << 1))
    for dq in range(16):
        greet(r, c ^ (2 * dq + 1))
    for dz in range(4):
        greet(r ^ 4, c ^ (2 * dz + 1))

    lane = lax.broadcasted_iota(jnp.int32, (1, 128), 1)
    low = lane < 64

    def half_lanes(a, b):
        return jnp.where(low, a, b)

    def swap(values):
        return pltpu.roll(values, 64, 1)

    for fetch in fetches:
        fetch.wait()

    flat = pair_ref[...].astype(F32).reshape(1024, 128)
    xf[...] = flat
    xn[...] = norm_over(flat, 1).astype(BF16).astype(F32)
    wpt[...] = flip(proj_ref[...])
    for k in range(16):
        part = xn[pl.ds(k, 64, stride=16), :].astype(BF16)
        nk[k] = jnp.concatenate([part, part], axis=0)

    two = mask_ref[pl.ds(r >> 1, 1), :].astype(F32)
    odd = (r & 1) == 1
    turned = swap(jnp.broadcast_to(two, (8, 128)))[0:1]
    row_live = half_lanes(jnp.where(odd, turned, two), jnp.where(odd, two, turned))
    col_live = [mask_smem[c * 16 + k].astype(F32) for k in range(16)]

    pl.semaphore_wait(barrier, 147)

    def project(step):
        to_y = y ^ 2 ^ step ^ (step >> 1)
        first = pl.multiple_of(to_y * 16, 16)
        weights = jnp.concatenate(
            [wpt[pl.ds(64 * b + first, 16), :] for b in range(8)], axis=0
        )
        for k in range(16):
            z = dot_nt(weights, nk[k])
            g = half_lanes(z[0:32], z[64:96])
            v = half_lanes(z[32:64], z[96:128])
            ms[pl.ds(k, 32, stride=16), :] = jax.nn.sigmoid(g) * v * (row_live * col_live[k])
        for zl in range(2):
            sb[zl, to_y] = ms[256 * zl : 256 * zl + 256, :].astype(BF16).reshape(16, 16, 128)

        def send(dx, dz):
            to_zl = half ^ (dz & 1)
            flips = dx << 2 | dz >> 1
            return pltpu.make_async_remote_copy(
                src_ref=sb.at[to_zl, to_y, q ^ flips],
                dst_ref=a_buf.at[p, r, q],
                send_sem=send1,
                recv_sem=recv1.at[r],
                device_id=(to_zl * 4 + to_y, c ^ (flips << 1)),
                device_id_type=MESH,
            )

        for dx in FAR4:
            for dz in FAR8:
                if dx or dz:
                    send(dx, dz).start()

        @pl.when(step < 3)
        def _():
            send(0, 0).start()

        @pl.when(step == 3)
        def _():
            pltpu.make_async_copy(sb.at[half, y, q], a_buf.at[p, r, q], recv1.at[r]).start()

    loop(0, 4, project)
    sent = [lambda: wait_bytes(sb.at[0], send1), lambda: wait_bytes(sb.at[0, pl.ds(0, 3)], send1)]
    sent.append(lambda: wait_bytes(sb.at[0, 0, pl.ds(0, 15)], send1))

    gate_t[...] = flip(gate_ref[...])
    tout_t[...] = flip(tout_ref[...])
    qkvg_t[...] = flip(qkvg_ref[...])

    def prepare(s):
        pos = jnp.concatenate(
            [xf[pl.ds(s, 64, stride=16), :], xf[pl.ds(s + 8, 64, stride=16), :]], axis=0
        )
        pt[s] = pos.T
        norm_pos = jnp.concatenate([nk[s, 0:64], nk[s + 8, 0:64]], axis=0)
        gt[s] = jax.nn.sigmoid(dot_nt(gate_t[...], norm_pos))

    loop(0, 8, prepare)

    def forward_copy(row):
        return pltpu.make_async_remote_copy(
            src_ref=a_buf.at[p, row],
            dst_ref=a_buf.at[p, row],
            send_sem=fsend.at[row],
            recv_sem=frecv.at[row],
            device_id=sibling,
            device_id_type=MESH,
        )

    def turn(core, row):
        part = flip(a_buf[core, row].reshape(256, 128))
        rt[core, pl.ds(pl.multiple_of(row * 64, 64), 64), :] = part[64:128]

    def arriving(step):
        pair = step >> 1
        return r ^ (2 ^ pair ^ (pair >> 1)) ^ ((step & 1) << 2)

    def forward(step):
        row = arriving(step)
        wait_bytes(a_buf.at[p, row], recv1.at[row])
        forward_copy(row).start()
        turn(p, row)

    loop(0, 8, forward)
    sent.append(lambda: loop(0, 8, lambda row: forward_copy(row).wait_send()))

    def turn_other(step):
        row = arriving(step)
        wait_bytes(a_buf.at[1 - p, row], frecv.at[row])
        turn(1 - p, row)

    loop(0, 8, turn_other)

    def triangle(step):
        to_y = y ^ 2 ^ step ^ (step >> 1)
        row = 4 * p + to_y
        prod = dot(rt[0], a_buf[0, row].reshape(256, 128))
        prod = (prod + dot(rt[1], a_buf[1, row].reshape(256, 128))).reshape(16, 2, 16, 128)
        hi = swap(prod[:, 1].reshape(256, 128)).reshape(16, 16, 128)
        s_buf[to_y] = jnp.where(low[None], prod[:, 0], hi).astype(BF16)

        def send(flips):
            return pltpu.make_async_remote_copy(
                src_ref=s_buf.at[to_y, q ^ flips],
                dst_ref=t_buf.at[chip],
                send_sem=send2,
                recv_sem=recv2.at[r],
                device_id=(row, c ^ (flips << 1)),
                device_id_type=MESH,
            )

        for dx in FAR4:
            for dz in FAR4:
                if dx or dz:
                    send(dx << 2 | dz).start()

        @pl.when(jnp.logical_or(step < 3, p != half))
        def _():
            send(0).start()

        @pl.when(jnp.logical_and(step == 3, p == half))
        def _():
            pltpu.make_async_copy(s_buf.at[to_y, q], t_buf.at[chip], recv2.at[r]).start()

    loop(0, 4, triangle)

    def triangle_sent():
        wait_bytes(s_buf.at[pl.ds(0, 3)], send2)
        wait_bytes(s_buf.at[0, pl.ds(0, 15)], send2)

        @pl.when(p != half)
        def _():
            wait_bytes(s_buf.at[0, 0], send2)

    sent.append(triangle_sent)

    def hand_copy(row):
        block = t_buf.at[pl.ds(pl.multiple_of(row * 16, 16), 16)]
        return pltpu.make_async_remote_copy(
            src_ref=block,
            dst_ref=block,
            send_sem=gsend.at[row],
            recv_sem=grecv.at[row],
            device_id=sibling,
            device_id_type=MESH,
        )

    def widen(row):
        block = t_buf[pl.ds(pl.multiple_of(row * 16, 16), 16)]
        tf[pl.ds(pl.multiple_of(row * 256, 256), 256), :] = block.astype(F32).reshape(256, 128)

    @pl.when(p == half)
    def _():
        def hand(step):
            row = arriving(step)
            wait_bytes(t_buf.at[pl.ds(pl.multiple_of(row * 16, 16), 16)], recv2.at[row])
            hand_copy(row).start()
            widen(row)

        loop(0, 8, hand)

    @pl.when(p != half)
    def _():
        def take(step):
            row = arriving(step)
            wait_bytes(t_buf.at[pl.ds(pl.multiple_of(row * 16, 16), 16)], grecv.at[row])
            widen(row)

        loop(0, 8, take)

    def handed():
        @pl.when(p == half)
        def _():
            loop(0, 8, lambda row: hand_copy(row).wait_send())

    sent.append(handed)

    def home(s):
        one = tf[pl.ds(s, 128, stride=16), :]
        two = tf[pl.ds(s + 8, 128, stride=16), :]
        mixed = swap(half_lanes(two, one))
        tri = half_lanes(jnp.where(p == 0, one, mixed), jnp.where(p == 0, mixed, two))
        tri_norm = norm_over(tri, 0).astype(BF16)
        updated = pt[s] + gt[s] * dot(tout_t[...], tri_norm)
        updt[s] = updated
        norm_two = norm_over(updated, 0)
        here = jnp.where(
            low, mask_smem[c * 16 + s].astype(F32), mask_smem[c * 16 + s + 8].astype(F32)
        )
        heads = dot(abias_ref[...], norm_two.astype(BF16))[0:4]
        bscr[pl.ds(s, 4, stride=8), :] = jnp.where(here > 0, heads, -1000000000.0)
        turned = norm_two.T
        n2s[pl.ds(s, 64, stride=16), :] = turned[0:64]
        n2s[pl.ds(s + 8, 64, stride=16), :] = turned[64:128]

    loop(0, 8, home, unroll=2)

    for pair in range(2):
        h0 = bscr[16 * pair : 16 * pair + 8, :]
        h1 = bscr[16 * pair + 8 : 16 * pair + 16, :]
        tile = jnp.concatenate([half_lanes(h0, swap(h1)), half_lanes(swap(h0), h1)], axis=0)
        bm[:, 128 * pair : 128 * pair + 128] = tile.astype(BF16)

    def bias_copy(src, dst, sem, recv, row, col):
        return pltpu.make_async_remote_copy(
            src_ref=src, dst_ref=dst, send_sem=bsend.at[sem], recv_sem=recv,
            device_id=(row, col), device_id_type=MESH,
        )

    def along_z(dz):
        to = (c ^ ((dz >> 1) << 1)) & 30 | half
        return bias_copy(bm, bias.at[p, y, x, zh], 0, bz, r ^ ((dz & 1) << 2), to)

    for dz in FAR8:
        if dz:
            along_z(dz).start()

    @pl.when(p == half)
    def _():
        pltpu.make_async_copy(bm, bias.at[p, y, x, zh], bz).start()

    @pl.when(p != half)
    def _():
        along_z(0).start()

    def bias_z_sent():
        wait_bytes(bias.at[0, 0, 0], bsend.at[0])
        wait_bytes(bias.at[0, 0, 0, pl.ds(0, 3)], bsend.at[0])

        @pl.when(p != half)
        def _():
            wait_bytes(bias.at[0, 0, 0, 0], bsend.at[0])

    sent.append(bias_z_sent)

    ns[...] = n2s[...].astype(BF16).reshape(64, 16, 128)

    for dx in FAR4:
        for dz in FAR4:
            flips = dx << 2 | dz
            if flips:
                pltpu.make_async_remote_copy(
                    src_ref=ns.at[pl.ds(4 * (q ^ flips), 4)],
                    dst_ref=x_buf.at[:, p, q],
                    send_sem=send3,
                    recv_sem=recv3,
                    device_id=(r, c ^ (flips << 1)),
                    device_id_type=MESH,
                ).start()
    pltpu.make_async_copy(ns.at[pl.ds(4 * q, 4)], x_buf.at[:, p, q], recv3).start()
    sent.append(lambda: wait_bytes(x_buf.at[:, 0, pl.ds(0, 15)], send3))

    wait_bytes(bias.at[:, 0, 0], bz)

    def second_x(dx):
        block = bias.at[0, y, x]
        return bias_copy(block, block, dx, ba, r, c ^ (dx << 3))

    def second_y(dy):
        block = bias.at[1, y, x]
        return bias_copy(block, block, 3 + dy, bb, r ^ dy, c)

    for d in FAR4[:3]:
        second_x(d).start()
        second_y(d).start()

    def third_y(dy):
        block = bias.at[0, y]
        return bias_copy(block, block, 6 + dy, bya, r ^ dy, c)

    def third_x(dx):
        block = bias.at[1, :, x]
        return bias_copy(block, block, 9 + dx, bxb, r, c ^ (dx << 3))

    wait_bytes(bias.at[0, 0, pl.ds(0, 3)], ba)
    for d in FAR4[:3]:
        third_y(d).start()
    wait_bytes(bias.at[1, pl.ds(0, 3), 0], bb)
    for d in FAR4[:3]:
        third_x(d).start()

    def bias_sent():
        for d in FAR4[:3]:
            second_x(d).wait_send()
            second_y(d).wait_send()
            third_y(d).wait_send()
            third_x(d).wait_send()

    sent.append(bias_sent)

    wait_bytes(x_buf.at[:, p], recv3)
    rows_swap = pltpu.make_async_remote_copy(
        src_ref=x_buf.at[:, p], dst_ref=x_buf.at[:, p], send_sem=xsend, recv_sem=xrecv,
        device_id=sibling, device_id_type=MESH,
    )
    rows_swap.start()
    sent.append(lambda: rows_swap.wait_send())

    def keys_values(core):
        def body(i):
            rows = x_buf[i, core].reshape(256, 128)
            kb[i, core] = dot(rows, qkvg_ref[:, 128:256]).astype(BF16)
            vt[i, core] = dot_nt(qkvg_t[256:384, :], rows).astype(BF16)

        loop(0, 4, body)

    keys_values(p)

    def restore(s):
        turned = updt[s].T
        up[pl.ds(s, 64, stride=16), :] = turned[0:64]
        up[pl.ds(s + 8, 64, stride=16), :] = turned[64:128]

    loop(0, 8, restore)

    wait_bytes(x_buf.at[:, p], xrecv)
    keys_values(1 - p)

    def queries_gate(i):
        mine = jnp.concatenate(
            [x_buf[i, core, 8 * p + chips] for chips in range(8) for core in range(2)], axis=0
        )
        qt[i] = dot_nt(qkvg_t[0:128, :], mine).astype(BF16).astype(F32)
        gq[i] = jax.nn.sigmoid(dot_nt(qkvg_t[384:512, :], mine))

    loop(0, 4, queries_gate)

    head_of_row = lax.broadcasted_iota(jnp.int32, (128, 128), 0) // 32
    head_of_lane = lax.broadcasted_iota(jnp.int32, (128, 128), 1) // 64
    scale = 1.0 / math.sqrt(32.0)

    wait_bytes(bias.at[0, pl.ds(0, 3)], bya)
    wait_bytes(bias.at[1, :, pl.ds(0, 3)], bxb)

    def attend(t):
        def row(i):
            x_t = qt[i, :, pl.ds(pl.multiple_of(128 * t, 128), 128)]
            x_s = swap(x_t)
            outs = []
            for e in range(2):
                d = half_lanes(x_t, x_s) if e == 0 else half_lanes(x_s, x_t)
                queries = jnp.concatenate(
                    [jnp.where(head_of_row == head_of_lane + 2 * pair, d, 0.0) for pair in range(2)],
                    axis=1,
                ).astype(BF16)
                scores = dot(kb[i].reshape(512, 128), queries) * scale
                scores = scores + bias[:, 2 * t + e].reshape(512, 256).astype(F32)
                exps = jnp.exp(scores - jnp.max(scores, axis=0, keepdims=True))
                weights = exps * (1.0 / jnp.sum(exps, axis=0, keepdims=True))
                weights = weights.astype(BF16)
                outs.append(dot(vt[i, 0], weights[0:256]) + dot(vt[i, 1], weights[256:512]))
            parts = []
            for h in range(4):
                at = (h // 2) * 128
                first = outs[0][32 * h : 32 * h + 32, at : at + 128]
                second = outs[1][32 * h : 32 * h + 32, at : at + 128]
                if h % 2 == 0:
                    parts.append(half_lanes(first, swap(second)))
                else:
                    parts.append(half_lanes(swap(first), second))
            attended = jnp.concatenate(parts, axis=0)
            gated = gq[i, :, pl.ds(pl.multiple_of(128 * t, 128), 128)] * attended
            gs[i, pl.ds(8 * t, 8)] = gated.T.astype(BF16).reshape(8, 16, 128)

        loop(0, 4, row)

        def send(off):
            cl = 8 * t + off
            to = 16 * p + cl

            @pl.when(to == c)
            def _():
                pltpu.make_async_copy(gs.at[:, cl], h_buf.at[pl.ds(4 * q, 4)], recv4).start()

            @pl.when(to != c)
            def _():
                pltpu.make_async_remote_copy(
                    src_ref=gs.at[:, cl],
                    dst_ref=h_buf.at[pl.ds(4 * q, 4)],
                    send_sem=send4,
                    recv_sem=recv4,
                    device_id=(r, to),
                    device_id_type=MESH,
                ).start()

        loop(0, 8, send)

    loop(0, 2, attend)

    def gated_sent():
        wait_bytes(gs.at[:, pl.ds(0, 15)], send4)

        @pl.when((c >> 4) != p)
        def _():
            wait_bytes(gs.at[:, 0], send4)

    sent.append(gated_sent)

    for wait in sent:
        wait()

    wait_bytes(h_buf, recv4)
    product = dot(h_buf[...].reshape(1024, 128), aout_ref[...])
    out_ref[...] = (up[...] + product).astype(BF16).reshape(64, 16, 128)


def local(pair_map, res_mask, tri_proj, tri_gate, tri_out, att_qkvg, att_bias, att_out):
    dma = pltpu.SemaphoreType.DMA
    return pl.pallas_call(
        kernel,
        out_shape=jax.ShapeDtypeStruct((64, 16, 128), BF16),
        in_specs=[pl.BlockSpec(memory_space=pltpu.HBM)] * 9,
        out_specs=pl.BlockSpec(memory_space=pltpu.VMEM),
        scratch_shapes=[
            pltpu.VMEM((64, 16, 128), BF16),
            pltpu.SMEM((512,), jnp.int32),
            pltpu.VMEM((4, 128), jnp.int32),
            pltpu.VMEM((128, 512), BF16),
            pltpu.VMEM((128, 128), BF16),
            pltpu.VMEM((128, 128), BF16),
            pltpu.VMEM((128, 512), BF16),
            pltpu.VMEM((4, 128), BF16),
            pltpu.VMEM((128, 128), BF16),
            dma((9,)),
            pltpu.VMEM((1024, 128), F32),
            pltpu.VMEM((1024, 128), F32),
            pltpu.VMEM((16, 128, 128), BF16),
            pltpu.VMEM((512, 128), BF16),
            pltpu.VMEM((512, 128), F32),
            pltpu.VMEM((2, 4, 16, 16, 128), BF16),
            pltpu.VMEM((8, 128, 128), F32),
            pltpu.VMEM((8, 128, 128), F32),
            pltpu.VMEM((128, 128), BF16),
            pltpu.VMEM((128, 128), BF16),
            pltpu.VMEM((512, 128), BF16),
            pltpu.VMEM((2, 8, 16, 16, 128), BF16),
            pltpu.VMEM((2, 512, 256), BF16),
            pltpu.VMEM((4, 16, 16, 128), BF16),
            pltpu.VMEM((128, 16, 128), BF16),
            pltpu.VMEM((2048, 128), F32),
            pltpu.VMEM((8, 128, 128), F32),
            pltpu.VMEM((1024, 128), F32),
            pltpu.VMEM((64, 16, 128), BF16),
            pltpu.VMEM((32, 128), F32),
            pltpu.VMEM((16, 256), BF16),
            pltpu.VMEM((1024, 128), F32),
            pltpu.VMEM((4, 2, 16, 16, 128), BF16),
            pltpu.VMEM((2, 4, 4, 4, 16, 256), BF16),
            pltpu.VMEM((4, 2, 256, 128), BF16),
            pltpu.VMEM((4, 2, 128, 256), BF16),
            pltpu.VMEM((4, 128, 256), F32),
            pltpu.VMEM((4, 128, 256), F32),
            pltpu.VMEM((4, 16, 16, 128), BF16),
            pltpu.VMEM((64, 16, 128), BF16),
            dma, dma((8,)),
            dma((8,)), dma((8,)),
            dma, dma((8,)),
            dma((8,)), dma((8,)),
            dma, dma,
            dma, dma,
            dma((13,)),
            dma, dma, dma, dma, dma,
            dma, dma,
        ],
        compiler_params=pltpu.CompilerParams(
            collective_id=0, has_side_effects=True, vmem_limit_bytes=60 * 1024 * 1024
        ),
    )(
        pair_map, res_mask, res_mask.reshape(4, 128), tri_proj, tri_gate, tri_out, att_qkvg,
        att_bias.T, att_out,
    )


def solution(mesh):
    in_specs = (P("row", "col", None), P(), P(), P(), P(), P(), P(), P())
    out_specs = P("row", "col", None)
    return jax.shard_map(local, mesh=mesh, in_specs=in_specs, out_specs=out_specs, check_vma=False)
```

time: 106 us -> 79.2 us (0.75)
  the two profiles are of different devices: /device:TPU:59 before, /device:TPU:3 now
where the time goes in v2:
time: 79.2 us; the launch traced here: 79.1 us
  Pallas kernels  77.4 us (98%)
  local copies, waits for them, and re-layouts  1.67 us (2%)
    pallas_call x1, Pallas kernels, local(): pl.pallas_call(kernel, out_shape=jax.ShapeDtypeStruct((64, 16, 128), BF16...  77.4 us
    unnamed x1, local copies, waits for them, and re-layouts  1.67 us

profile of v2, /device:TPU:3, one launch (start us, length us, event | category | flops | bytes accessed | tf_op | source)
XLA Modules:
  0.0 79.1 jit_solution(18129040040297136567)
XLA Ops:
  0.0 77.4 %shard_map.82 = bf16[64,16,128]{2,1,0:T(8,128)(2,1)} custom-call(bf16[64,16,128]{2,1,0:T(8,128)(2,1)} %pair_hbm.1, s32[512]{0:T(512)} %mask_hbm.1, s32[4,128]{1,0:T(4,128)} %bitcast.2, bf16[128,512]{1,0:T(8,128)(2,1)} %proj_hbm.1, bf16[128,128]{1,0:T(8,128)(2,1)} %gate_hbm.1, bf16[128,128]{1,0:T(8,128)(2,1)} %tout_hbm.1, bf16[128,512]{1,0:T(8,128)(2,1)} %qkvg_hbm.1, ...), custom_call_target="tpu_custom_call" | custom-call | tf_op jit(solution)/shard_map/pallas_call | solution.py:532
  77.5 1.7 %copy.10 = bf16[64,16,128]{2,1,0:T(8,128)(2,1)} copy(bf16[64,16,128]{2,1,0:T(8,128)(2,1)} %shard_map.82) | data formatting | bytes 524288

commit v3 on v2

--- a/solution.py
+++ b/solution.py
@@ -51,10 +51,10 @@
     out_ref,
     pair_ref, mask_smem, mask_ref, proj_ref, gate_ref, tout_ref, qkvg_ref, abias_ref, aout_ref, loads,
     xf, xn, nk, wpt, ms, sb, pt, gt, gate_t, tout_t, qkvg_t,
-    a_buf, rt, s_buf, t_buf, tf, updt, n2s, ns, bscr, bm, up,
-    x_buf, bias, kb, vt, qt, gq, gs, h_buf,
+    a_buf, rt, s_buf, t_buf, tf, updt, n2t, n2s, ns, bscr, bm, up,
+    x_buf, bias, kb, vt, qb, gq, bf, sc, wb, oscr, gs, h_buf,
     send1, recv1, fsend, frecv, send2, recv2, gsend, grecv, send3, recv3, xsend, xrecv,
-    bsend, bz, ba, bb, bya, bxb, send4, recv4,
+    bsend, bz, bu, send4, recv4,
 ):
     r = lax.axis_index("row")
     c = lax.axis_index("col")
@@ -312,9 +312,7 @@
         )
         heads = dot(abias_ref[...], norm_two.astype(BF16))[0:4]
         bscr[pl.ds(s, 4, stride=8), :] = jnp.where(here > 0, heads, -1000000000.0)
-        turned = norm_two.T
-        n2s[pl.ds(s, 64, stride=16), :] = turned[0:64]
-        n2s[pl.ds(s + 8, 64, stride=16), :] = turned[64:128]
+        n2t[s] = norm_two
 
     loop(0, 8, home, unroll=2)
 
@@ -356,6 +354,15 @@
 
     sent.append(bias_z_sent)
 
+    def rows_of(source, target):
+        def body(s):
+            turned = source[s].T
+            target[pl.ds(s, 64, stride=16), :] = turned[0:64]
+            target[pl.ds(s + 8, 64, stride=16), :] = turned[64:128]
+
+        loop(0, 8, body, unroll=2)
+
+    rows_of(n2t, n2s)
     ns[...] = n2s[...].astype(BF16).reshape(64, 16, 128)
 
     for dx in FAR4:
@@ -373,41 +380,34 @@
     pltpu.make_async_copy(ns.at[pl.ds(4 * q, 4)], x_buf.at[:, p, q], recv3).start()
     sent.append(lambda: wait_bytes(x_buf.at[:, 0, pl.ds(0, 15)], send3))
 
+    rows_of(updt, up)
+
+    def unit_copy(core, unit_y, unit_x, dy, dx):
+        unit = bias.at[core, unit_y, unit_x]
+        return bias_copy(unit, unit, 1, bu.at[core, unit_y, unit_x], r ^ dy, c ^ (dx << 3))
+
+    def unit_wait(core, unit_y, unit_x):
+        wait_bytes(bias.at[core, unit_y, unit_x], bu.at[core, unit_y, unit_x])
+
     wait_bytes(bias.at[:, 0, 0], bz)
-
-    def second_x(dx):
-        block = bias.at[0, y, x]
-        return bias_copy(block, block, dx, ba, r, c ^ (dx << 3))
-
-    def second_y(dy):
-        block = bias.at[1, y, x]
-        return bias_copy(block, block, 3 + dy, bb, r ^ dy, c)
-
     for d in FAR4[:3]:
-        second_x(d).start()
-        second_y(d).start()
-
-    def third_y(dy):
-        block = bias.at[0, y]
-        return bias_copy(block, block, 6 + dy, bya, r ^ dy, c)
-
-    def third_x(dx):
-        block = bias.at[1, :, x]
-        return bias_copy(block, block, 9 + dx, bxb, r, c ^ (dx << 3))
-
-    wait_bytes(bias.at[0, 0, pl.ds(0, 3)], ba)
+        unit_copy(0, y, x, 0, d).start()
+        unit_copy(1, y, x, d, 0).start()
     for d in FAR4[:3]:
-        third_y(d).start()
-    wait_bytes(bias.at[1, pl.ds(0, 3), 0], bb)
-    for d in FAR4[:3]:
-        third_x(d).start()
+        unit_copy(0, y, x, d, 0).start()
+        unit_copy(1, y, x, 0, d).start()
+    for near in (1, 3, 2):
+        unit_wait(0, y, x ^ near)
+        for d in FAR4[:3]:
+            unit_copy(0, y, x ^ near, d, 0).start()
+        unit_wait(1, y ^ near, x)
+        for d in FAR4[:3]:
+            unit_copy(1, y ^ near, x, 0, d).start()
 
     def bias_sent():
-        for d in FAR4[:3]:
-            second_x(d).wait_send()
-            second_y(d).wait_send()
-            third_y(d).wait_send()
-            third_x(d).wait_send()
+        wait_bytes(bias.at[0], bsend.at[1])
+        wait_bytes(bias.at[1, pl.ds(0, 3)], bsend.at[1])
+        wait_bytes(bias.at[1, 0, pl.ds(0, 2)], bsend.at[1])
 
     sent.append(bias_sent)
 
@@ -423,69 +423,104 @@
         def body(i):
             rows = x_buf[i, core].reshape(256, 128)
             kb[i, core] = dot(rows, qkvg_ref[:, 128:256]).astype(BF16)
-            vt[i, core] = dot_nt(qkvg_t[256:384, :], rows).astype(BF16)
+            vt[i, :, pl.ds(pl.multiple_of(256 * core, 256), 256)] = dot_nt(
+                qkvg_t[256:384, :], rows
+            ).astype(BF16)
 
         loop(0, 4, body)
 
     keys_values(p)
-
-    def restore(s):
-        turned = updt[s].T
-        up[pl.ds(s, 64, stride=16), :] = turned[0:64]
-        up[pl.ds(s + 8, 64, stride=16), :] = turned[64:128]
-
-    loop(0, 8, restore)
-
     wait_bytes(x_buf.at[:, p], xrecv)
     keys_values(1 - p)
+
+    head_of_row = lax.broadcasted_iota(jnp.int32, (128, 128), 0) // 32
+    head_of_lane = lax.broadcasted_iota(jnp.int32, (128, 128), 1) // 64
 
     def queries_gate(i):
         mine = jnp.concatenate(
             [x_buf[i, core, 8 * p + chips] for chips in range(8) for core in range(2)], axis=0
         )
-        qt[i] = dot_nt(qkvg_t[0:128, :], mine).astype(BF16).astype(F32)
+        queries = dot_nt(qkvg_t[0:128, :], mine).astype(BF16).astype(F32)
         gq[i] = jax.nn.sigmoid(dot_nt(qkvg_t[384:512, :], mine))
+        for unit_y in range(4):
+            q_t = queries[:, 128 * (unit_y // 2) : 128 * (unit_y // 2) + 128]
+            q_s = swap(q_t)
+            both = half_lanes(q_t, q_s) if unit_y % 2 == 0 else half_lanes(q_s, q_t)
+            for pair in range(2):
+                qb[i, unit_y, :, 128 * pair : 128 * pair + 128] = jnp.where(
+                    head_of_row == head_of_lane + 2 * pair, both, 0.0
+                ).astype(BF16)
 
     loop(0, 4, queries_gate)
 
-    head_of_row = lax.broadcasted_iota(jnp.int32, (128, 128), 0) // 32
-    head_of_lane = lax.broadcasted_iota(jnp.int32, (128, 128), 1) // 64
-    scale = 1.0 / math.sqrt(32.0)
-
-    wait_bytes(bias.at[0, pl.ds(0, 3)], bya)
-    wait_bytes(bias.at[1, :, pl.ds(0, 3)], bxb)
-
-    def attend(t):
-        def row(i):
-            x_t = qt[i, :, pl.ds(pl.multiple_of(128 * t, 128), 128)]
-            x_s = swap(x_t)
-            outs = []
-            for e in range(2):
-                d = half_lanes(x_t, x_s) if e == 0 else half_lanes(x_s, x_t)
-                queries = jnp.concatenate(
-                    [jnp.where(head_of_row == head_of_lane + 2 * pair, d, 0.0) for pair in range(2)],
-                    axis=1,
-                ).astype(BF16)
-                scores = dot(kb[i].reshape(512, 128), queries) * scale
-                scores = scores + bias[:, 2 * t + e].reshape(512, 256).astype(F32)
-                exps = jnp.exp(scores - jnp.max(scores, axis=0, keepdims=True))
-                weights = exps * (1.0 / jnp.sum(exps, axis=0, keepdims=True))
-                weights = weights.astype(BF16)
-                outs.append(dot(vt[i, 0], weights[0:256]) + dot(vt[i, 1], weights[256:512]))
-            parts = []
+    log2e = 1.0 / math.log(2.0)
+    scale = log2e / math.sqrt(32.0)
+
+    def scores_of(i, unit_y, at, highest):
+        core, first = at // 4, 64 * (at % 4)
+        part = dot(kb[i, core, first : first + 64, :], qb[i, unit_y]) * scale
+        part = part + bf[64 * at : 64 * at + 64, :]
+        sc[i % 2, 64 * at : 64 * at + 64, :] = part
+        top = jnp.max(part.reshape(8, 8, 256), axis=0)
+        return top if highest is None else jnp.maximum(highest, top)
+
+    def exps_of(i, at, highest, total):
+        part = jnp.exp2(sc[i % 2, 64 * at : 64 * at + 64, :] - highest)
+        wb[i % 2, 64 * at : 64 * at + 64, :] = part.astype(BF16)
+        here = jnp.sum(part.reshape(8, 8, 256), axis=0)
+        return here if total is None else total + here
+
+    def block(step):
+        unit_y = y ^ step ^ (step >> 1)
+
+        @pl.when(step == 0)
+        def _():
+            for d in (1, 3, 2):
+                unit_wait(1, y, x ^ d)
+
+        @pl.when(step > 0)
+        def _():
+            unit_wait(0, unit_y, x)
+            for d in (1, 3, 2):
+                unit_wait(0, unit_y, x ^ d)
+                unit_wait(1, unit_y, x ^ d)
+
+        for core in range(2):
+            bf[256 * core : 256 * core + 256, :] = (
+                bias[core, unit_y].reshape(256, 256).astype(F32) * log2e
+            )
+        highest = None
+        for at in range(8):
+            highest = scores_of(0, unit_y, at, highest)
+        for i in range(4):
+            top = jnp.max(highest, axis=0, keepdims=True)
+            highest = total = None
+            for at in range(8):
+                if i < 3:
+                    highest = scores_of(i + 1, unit_y, at, highest)
+                total = exps_of(i, at, top, total)
+            inverse = 1.0 / jnp.sum(total, axis=0, keepdims=True)
+            out = dot(vt[i], wb[i % 2]) * inverse
             for h in range(4):
                 at = (h // 2) * 128
-                first = outs[0][32 * h : 32 * h + 32, at : at + 128]
-                second = outs[1][32 * h : 32 * h + 32, at : at + 128]
-                if h % 2 == 0:
-                    parts.append(half_lanes(first, swap(second)))
-                else:
-                    parts.append(half_lanes(swap(first), second))
-            attended = jnp.concatenate(parts, axis=0)
+                oscr[i, unit_y, 32 * h : 32 * h + 32, :] = out[32 * h : 32 * h + 32, at : at + 128]
+
+    odd_head = (head_of_row & 1) == 1
+
+    def attend(turn_of):
+        loop(2 * turn_of, 2 * turn_of + 2, block)
+        t = (y >> 1) ^ turn_of
+
+        def finish(i):
+            first = oscr[i, 2 * t]
+            second = oscr[i, 2 * t + 1]
+            attended = half_lanes(
+                jnp.where(odd_head, swap(first), first), jnp.where(odd_head, second, swap(second))
+            )
             gated = gq[i, :, pl.ds(pl.multiple_of(128 * t, 128), 128)] * attended
             gs[i, pl.ds(8 * t, 8)] = gated.T.astype(BF16).reshape(8, 16, 128)
 
-        loop(0, 4, row)
+        loop(0, 4, finish, unroll=2)
 
         def send(off):
             cl = 8 * t + off
@@ -562,6 +597,7 @@
             pltpu.VMEM((128, 16, 128), BF16),
             pltpu.VMEM((2048, 128), F32),
             pltpu.VMEM((8, 128, 128), F32),
+            pltpu.VMEM((8, 128, 128), F32),
             pltpu.VMEM((1024, 128), F32),
             pltpu.VMEM((64, 16, 128), BF16),
             pltpu.VMEM((32, 128), F32),
@@ -570,9 +606,13 @@
             pltpu.VMEM((4, 2, 16, 16, 128), BF16),
             pltpu.VMEM((2, 4, 4, 4, 16, 256), BF16),
             pltpu.VMEM((4, 2, 256, 128), BF16),
-            pltpu.VMEM((4, 2, 128, 256), BF16),
+            pltpu.VMEM((4, 128, 512), BF16),
+            pltpu.VMEM((4, 4, 128, 256), BF16),
             pltpu.VMEM((4, 128, 256), F32),
-            pltpu.VMEM((4, 128, 256), F32),
+            pltpu.VMEM((512, 256), F32),
+            pltpu.VMEM((2, 512, 256), F32),
+            pltpu.VMEM((2, 512, 256), BF16),
+            pltpu.VMEM((4, 4, 128, 128), F32),
             pltpu.VMEM((4, 16, 16, 128), BF16),
             pltpu.VMEM((64, 16, 128), BF16),
             dma, dma((8,)),
@@ -581,8 +621,8 @@
             dma((8,)), dma((8,)),
             dma, dma,
             dma, dma,
-            dma((13,)),
-            dma, dma, dma, dma, dma,
+            dma((2,)),
+            dma, dma((2, 4, 4)),
             dma, dma,
         ],
         compiler_params=pltpu.CompilerParams(

time: 79.2 us -> 71.9 us (0.908)
  Pallas kernels: 77.4 us -> 70.1 us
    pallas_call x1, Pallas kernels: 77.4 us -> 70.1 us  [local(): pl.pallas_call(kernel, out_shape=jax.ShapeDtypeStruct((64, 16, 128), BF16...]
where the time goes in v3:
time: 71.9 us; the launch traced here: 71.8 us
  Pallas kernels  70.1 us (97%)
  local copies, waits for them, and re-layouts  1.67 us (2%)
    pallas_call x1, Pallas kernels, local(): pl.pallas_call(kernel, out_shape=jax.ShapeDtypeStruct((64, 16, 128), BF16...  70.1 us
    unnamed x1, local copies, waits for them, and re-layouts  1.67 us

profile of v3, /device:TPU:3, one launch (start us, length us, event | category | flops | bytes accessed | tf_op | source)
XLA Modules:
  0.0 71.8 jit_solution(13662185091665411473)
XLA Ops:
  0.0 70.1 %shard_map.82 = bf16[64,16,128]{2,1,0:T(8,128)(2,1)} custom-call(bf16[64,16,128]{2,1,0:T(8,128)(2,1)} %pair_hbm.1, s32[512]{0:T(512)} %mask_hbm.1, s32[4,128]{1,0:T(4,128)} %bitcast.2, bf16[128,512]{1,0:T(8,128)(2,1)} %proj_hbm.1, bf16[128,128]{1,0:T(8,128)(2,1)} %gate_hbm.1, bf16[128,128]{1,0:T(8,128)(2,1)} %tout_hbm.1, bf16[128,512]{1,0:T(8,128)(2,1)} %qkvg_hbm.1, ...), custom_call_target="tpu_custom_call" | custom-call | tf_op jit(solution)/shard_map/pallas_call | solution.py:567
  70.1 1.7 %copy.10 = bf16[64,16,128]{2,1,0:T(8,128)(2,1)} copy(bf16[64,16,128]{2,1,0:T(8,128)(2,1)} %shard_map.82) | data formatting | bytes 524288

commit v4 on v3

--- a/solution.py
+++ b/solution.py
@@ -13,6 +13,7 @@
 BF16 = jnp.bfloat16
 NT = (((1,), (1,)), ((), ()))
 FAR4 = (2, 3, 1, 0)
+CHUNK = 128
 FAR8 = (4, 5, 7, 3, 6, 2, 1, 0)
 
 
@@ -52,7 +53,7 @@
     pair_ref, mask_smem, mask_ref, proj_ref, gate_ref, tout_ref, qkvg_ref, abias_ref, aout_ref, loads,
     xf, xn, nk, wpt, ms, sb, pt, gt, gate_t, tout_t, qkvg_t,
     a_buf, rt, s_buf, t_buf, tf, updt, n2t, n2s, ns, bscr, bm, up,
-    x_buf, bias, kb, vt, qb, gq, bf, sc, wb, oscr, gs, h_buf,
+    x_buf, bias, kb, vt, qb, gq, bf, sc, wb, gs, h_buf,
     send1, recv1, fsend, frecv, send2, recv2, gsend, grecv, send3, recv3, xsend, xrecv,
     bsend, bz, bu, send4, recv4,
 ):
@@ -212,7 +213,7 @@
         wait_bytes(a_buf.at[1 - p, row], frecv.at[row])
         turn(1 - p, row)
 
-    loop(0, 8, turn_other)
+    loop(0, 8, turn_other, unroll=4)
 
     def triangle(step):
         to_y = y ^ 2 ^ step ^ (step >> 1)
@@ -245,7 +246,7 @@
         def _():
             pltpu.make_async_copy(s_buf.at[to_y, q], t_buf.at[chip], recv2.at[r]).start()
 
-    loop(0, 4, triangle)
+    loop(0, 4, triangle, unroll=4)
 
     def triangle_sent():
         wait_bytes(s_buf.at[pl.ds(0, 3)], send2)
@@ -280,7 +281,7 @@
             hand_copy(row).start()
             widen(row)
 
-        loop(0, 8, hand)
+        loop(0, 8, hand, unroll=4)
 
     @pl.when(p != half)
     def _():
@@ -289,7 +290,7 @@
             wait_bytes(t_buf.at[pl.ds(pl.multiple_of(row * 16, 16), 16)], grecv.at[row])
             widen(row)
 
-        loop(0, 8, take)
+        loop(0, 8, take, unroll=4)
 
     def handed():
         @pl.when(p == half)
@@ -314,7 +315,7 @@
         bscr[pl.ds(s, 4, stride=8), :] = jnp.where(here > 0, heads, -1000000000.0)
         n2t[s] = norm_two
 
-    loop(0, 8, home, unroll=2)
+    loop(0, 8, home, unroll=4)
 
     for pair in range(2):
         h0 = bscr[16 * pair : 16 * pair + 8, :]
@@ -360,23 +361,24 @@
             target[pl.ds(s, 64, stride=16), :] = turned[0:64]
             target[pl.ds(s + 8, 64, stride=16), :] = turned[64:128]
 
-        loop(0, 8, body, unroll=2)
+        loop(0, 8, body, unroll=4)
 
     rows_of(n2t, n2s)
     ns[...] = n2s[...].astype(BF16).reshape(64, 16, 128)
 
+    def rows_send(dx, dz):
+        flips = dx << 2 | dz
+        pltpu.make_async_remote_copy(
+            src_ref=ns.at[pl.ds(4 * (q ^ flips), 4)],
+            dst_ref=x_buf.at[:, p, q],
+            send_sem=send3,
+            recv_sem=recv3,
+            device_id=(r, c ^ (flips << 1)),
+            device_id_type=MESH,
+        ).start()
+
     for dx in FAR4:
-        for dz in FAR4:
-            flips = dx << 2 | dz
-            if flips:
-                pltpu.make_async_remote_copy(
-                    src_ref=ns.at[pl.ds(4 * (q ^ flips), 4)],
-                    dst_ref=x_buf.at[:, p, q],
-                    send_sem=send3,
-                    recv_sem=recv3,
-                    device_id=(r, c ^ (flips << 1)),
-                    device_id_type=MESH,
-                ).start()
+        rows_send(dx, 2)
     pltpu.make_async_copy(ns.at[pl.ds(4 * q, 4)], x_buf.at[:, p, q], recv3).start()
     sent.append(lambda: wait_bytes(x_buf.at[:, 0, pl.ds(0, 15)], send3))
 
@@ -390,19 +392,24 @@
         wait_bytes(bias.at[core, unit_y, unit_x], bu.at[core, unit_y, unit_x])
 
     wait_bytes(bias.at[:, 0, 0], bz)
-    for d in FAR4[:3]:
+    for d in (1, 3, 2):
         unit_copy(0, y, x, 0, d).start()
+        unit_copy(1, y, x, 0, d).start()
+    for dz in (3, 1, 0):
+        for dx in FAR4:
+            if dz or dx:
+                rows_send(dx, dz)
+    for d in (1, 3, 2):
+        unit_copy(0, y, x, d, 0).start()
         unit_copy(1, y, x, d, 0).start()
-    for d in FAR4[:3]:
-        unit_copy(0, y, x, d, 0).start()
-        unit_copy(1, y, x, 0, d).start()
     for near in (1, 3, 2):
         unit_wait(0, y, x ^ near)
-        for d in FAR4[:3]:
-            unit_copy(0, y, x ^ near, d, 0).start()
-        unit_wait(1, y ^ near, x)
-        for d in FAR4[:3]:
-            unit_copy(1, y ^ near, x, 0, d).start()
+    for dy in (1, 3, 2):
+        for near in (1, 3, 2):
+            unit_copy(0, y, x ^ near, dy, 0).start()
+        unit_wait(1, y ^ dy, x)
+        for dx in (1, 3, 2):
+            unit_copy(1, y ^ dy, x, 0, dx).start()
 
     def bias_sent():
         wait_bytes(bias.at[0], bsend.at[1])
@@ -427,7 +434,7 @@
                 qkvg_t[256:384, :], rows
             ).astype(BF16)
 
-        loop(0, 4, body)
+        loop(0, 4, body, unroll=4)
 
     keys_values(p)
     wait_bytes(x_buf.at[:, p], xrecv)
@@ -436,39 +443,60 @@
     head_of_row = lax.broadcasted_iota(jnp.int32, (128, 128), 0) // 32
     head_of_lane = lax.broadcasted_iota(jnp.int32, (128, 128), 1) // 64
 
-    def queries_gate(i):
-        mine = jnp.concatenate(
-            [x_buf[i, core, 8 * p + chips] for chips in range(8) for core in range(2)], axis=0
-        )
-        queries = dot_nt(qkvg_t[0:128, :], mine).astype(BF16).astype(F32)
-        gq[i] = jax.nn.sigmoid(dot_nt(qkvg_t[384:512, :], mine))
+    def queries_gate(pair_i):
+        gates = []
+        for i in (2 * pair_i, 2 * pair_i + 1):
+            mine = jnp.concatenate(
+                [x_buf[i, core, 8 * p + chips] for chips in range(8) for core in range(2)], axis=0
+            )
+            queries = dot_nt(qkvg_t[0:128, :], mine).astype(BF16).astype(F32)
+            gates.append(jax.nn.sigmoid(dot_nt(qkvg_t[384:512, :], mine)))
+            for unit_y in range(4):
+                q_t = queries[:, 128 * (unit_y // 2) : 128 * (unit_y // 2) + 128]
+                q_s = swap(q_t)
+                both = half_lanes(q_t, q_s) if unit_y % 2 == 0 else half_lanes(q_s, q_t)
+                for pair in range(2):
+                    qb[i, unit_y, :, 128 * pair : 128 * pair + 128] = jnp.where(
+                        head_of_row == head_of_lane + 2 * pair, both, 0.0
+                    ).astype(BF16)
         for unit_y in range(4):
-            q_t = queries[:, 128 * (unit_y // 2) : 128 * (unit_y // 2) + 128]
-            q_s = swap(q_t)
-            both = half_lanes(q_t, q_s) if unit_y % 2 == 0 else half_lanes(q_s, q_t)
-            for pair in range(2):
-                qb[i, unit_y, :, 128 * pair : 128 * pair + 128] = jnp.where(
-                    head_of_row == head_of_lane + 2 * pair, both, 0.0
-                ).astype(BF16)
-
-    loop(0, 4, queries_gate)
+            at = 128 * (unit_y // 2)
+            one, two = (gate[:, at : at + 128] for gate in gates)
+            gq[pair_i, unit_y] = (
+                half_lanes(one, swap(two)) if unit_y % 2 == 0 else half_lanes(swap(one), two)
+            )
+
+    for pair_i in range(2):
+        queries_gate(pair_i)
 
     log2e = 1.0 / math.log(2.0)
     scale = log2e / math.sqrt(32.0)
 
     def scores_of(i, unit_y, at, highest):
-        core, first = at // 4, 64 * (at % 4)
-        part = dot(kb[i, core, first : first + 64, :], qb[i, unit_y]) * scale
-        part = part + bf[64 * at : 64 * at + 64, :]
-        sc[i % 2, 64 * at : 64 * at + 64, :] = part
-        top = jnp.max(part.reshape(8, 8, 256), axis=0)
+        core, first = CHUNK * at // 256, CHUNK * at % 256
+        part = dot(kb[i, core, first : first + CHUNK, :], qb[i, unit_y]) * scale
+        part = part + bf[CHUNK * at : CHUNK * at + CHUNK, :]
+        sc[i % 2, CHUNK * at : CHUNK * at + CHUNK, :] = part
+        top = jnp.max(part.reshape(CHUNK // 8, 8, 256), axis=0)
         return top if highest is None else jnp.maximum(highest, top)
 
     def exps_of(i, at, highest, total):
-        part = jnp.exp2(sc[i % 2, 64 * at : 64 * at + 64, :] - highest)
-        wb[i % 2, 64 * at : 64 * at + 64, :] = part.astype(BF16)
-        here = jnp.sum(part.reshape(8, 8, 256), axis=0)
+        part = jnp.exp2(sc[i % 2, CHUNK * at : CHUNK * at + CHUNK, :] - highest)
+        wb[i % 2, CHUNK * at : CHUNK * at + CHUNK, :] = part.astype(BF16)
+        here = jnp.sum(part.reshape(CHUNK // 8, 8, 256), axis=0)
         return here if total is None else total + here
+
+    odd_head = (head_of_row & 1) == 1
+
+    def finish(pair_i, unit_y, first, second):
+        attended = half_lanes(
+            jnp.where(odd_head, swap(first), first), jnp.where(odd_head, second, swap(second))
+        )
+        gated = (gq[pair_i, unit_y] * attended).T.astype(BF16)
+        for own in range(2):
+            gs[2 * pair_i + own, pl.ds(4 * unit_y, 4)] = gated[64 * own : 64 * own + 64].reshape(
+                4, 16, 128
+            )
 
     def block(step):
         unit_y = y ^ step ^ (step >> 1)
@@ -490,60 +518,53 @@
                 bias[core, unit_y].reshape(256, 256).astype(F32) * log2e
             )
         highest = None
-        for at in range(8):
+        for at in range(512 // CHUNK):
             highest = scores_of(0, unit_y, at, highest)
+        outs = []
         for i in range(4):
             top = jnp.max(highest, axis=0, keepdims=True)
             highest = total = None
-            for at in range(8):
+            for at in range(512 // CHUNK):
                 if i < 3:
                     highest = scores_of(i + 1, unit_y, at, highest)
                 total = exps_of(i, at, top, total)
             inverse = 1.0 / jnp.sum(total, axis=0, keepdims=True)
             out = dot(vt[i], wb[i % 2]) * inverse
-            for h in range(4):
-                at = (h // 2) * 128
-                oscr[i, unit_y, 32 * h : 32 * h + 32, :] = out[32 * h : 32 * h + 32, at : at + 128]
-
-    odd_head = (head_of_row & 1) == 1
-
-    def attend(turn_of):
-        loop(2 * turn_of, 2 * turn_of + 2, block)
-        t = (y >> 1) ^ turn_of
-
-        def finish(i):
-            first = oscr[i, 2 * t]
-            second = oscr[i, 2 * t + 1]
-            attended = half_lanes(
-                jnp.where(odd_head, swap(first), first), jnp.where(odd_head, second, swap(second))
-            )
-            gated = gq[i, :, pl.ds(pl.multiple_of(128 * t, 128), 128)] * attended
-            gs[i, pl.ds(8 * t, 8)] = gated.T.astype(BF16).reshape(8, 16, 128)
-
-        loop(0, 4, finish, unroll=2)
-
-        def send(off):
-            cl = 8 * t + off
-            to = 16 * p + cl
-
-            @pl.when(to == c)
-            def _():
-                pltpu.make_async_copy(gs.at[:, cl], h_buf.at[pl.ds(4 * q, 4)], recv4).start()
-
-            @pl.when(to != c)
-            def _():
-                pltpu.make_async_remote_copy(
-                    src_ref=gs.at[:, cl],
-                    dst_ref=h_buf.at[pl.ds(4 * q, 4)],
-                    send_sem=send4,
-                    recv_sem=recv4,
-                    device_id=(r, to),
-                    device_id_type=MESH,
-                ).start()
-
-        loop(0, 8, send)
-
-    loop(0, 2, attend)
+            outs.append(
+                jnp.concatenate(
+                    [
+                        out[32 * h : 32 * h + 32, 128 * (h // 2) : 128 * (h // 2) + 128]
+                        for h in range(4)
+                    ],
+                    axis=0,
+                )
+            )
+            if i % 2 == 1:
+                finish(i // 2, unit_y, outs[i - 1], outs[i])
+
+        for off in range(4):
+            cl = 4 * unit_y + off
+            send_gated(cl)
+
+    def send_gated(cl):
+        to = 16 * p + cl
+
+        @pl.when(to == c)
+        def _():
+            pltpu.make_async_copy(gs.at[:, cl], h_buf.at[pl.ds(4 * q, 4)], recv4).start()
+
+        @pl.when(to != c)
+        def _():
+            pltpu.make_async_remote_copy(
+                src_ref=gs.at[:, cl],
+                dst_ref=h_buf.at[pl.ds(4 * q, 4)],
+                send_sem=send4,
+                recv_sem=recv4,
+                device_id=(r, to),
+                device_id_type=MESH,
+            ).start()
+
+    loop(0, 4, block)
 
     def gated_sent():
         wait_bytes(gs.at[:, pl.ds(0, 15)], send4)
@@ -608,11 +629,10 @@
             pltpu.VMEM((4, 2, 256, 128), BF16),
             pltpu.VMEM((4, 128, 512), BF16),
             pltpu.VMEM((4, 4, 128, 256), BF16),
-            pltpu.VMEM((4, 128, 256), F32),
+            pltpu.VMEM((2, 4, 128, 128), F32),
             pltpu.VMEM((512, 256), F32),
             pltpu.VMEM((2, 512, 256), F32),
             pltpu.VMEM((2, 512, 256), BF16),
-            pltpu.VMEM((4, 4, 128, 128), F32),
             pltpu.VMEM((4, 16, 16, 128), BF16),
             pltpu.VMEM((64, 16, 128), BF16),
             dma, dma((8,)),
@@ -626,11 +646,16 @@
             dma, dma,
         ],
         compiler_params=pltpu.CompilerParams(
-            collective_id=0, has_side_effects=True, vmem_limit_bytes=60 * 1024 * 1024
+            collective_id=0, has_side_effects=True, vmem_limit_bytes=48 * 1024 * 1024
         ),
     )(
-        pair_map, res_mask, res_mask.reshape(4, 128), tri_proj, tri_gate, tri_out, att_qkvg,
-        att_bias.T, att_out,
+        *(
+            pltpu.with_memory_space_constraint(operand, pltpu.HBM)
+            for operand in (
+                pair_map, res_mask, res_mask.reshape(4, 128), tri_proj, tri_gate, tri_out, att_qkvg,
+                att_bias.T, att_out,
+            )
+        )
     )
 
 

time: 71.9 us -> 67.6 us (0.940)
  Pallas kernels: 70.1 us -> 66.8 us
  local copies, waits for them, and re-layouts: 1.67 us -> 0.71 us
    pallas_call x1, Pallas kernels: 70.1 us -> 66.8 us  [local(): pl.pallas_call(kernel, out_shape=jax.ShapeDtypeStruct((64, 16, 128), BF16...]
    unnamed x1, local copies, waits for them, and re-layouts: 1.67 us -> 0.71 us
where the time goes in v4:
time: 67.6 us; the launch traced here: 67.5 us
  Pallas kernels  66.8 us (99%)
  local copies, waits for them, and re-layouts  0.71 us (1%)
    pallas_call x1, Pallas kernels, local(): pl.pallas_call(kernel, out_shape=jax.ShapeDtypeStruct((64, 16, 128), BF16...  66.8 us

profile of v4, /device:TPU:3, one launch (start us, length us, event | category | flops | bytes accessed | tf_op | source)
XLA Modules:
  0.0 67.5 jit_solution(13415465334297374349)
XLA Ops:
  0.0 66.8 %shard_map.82 = bf16[64,16,128]{2,1,0:T(8,128)(2,1)S(1)} custom-call(bf16[64,16,128]{2,1,0:T(8,128)(2,1)} %pair_hbm.1, s32[512]{0:T(512)} %mask_hbm.1, s32[4,128]{1,0:T(4,128)} %bitcast.2, bf16[128,512]{1,0:T(8,128)(2,1)} %proj_hbm.1, bf16[128,128]{1,0:T(8,128)(2,1)} %gate_hbm.1, bf16[128,128]{1,0:T(8,128)(2,1)} %tout_hbm.1, bf16[128,512]{1,0:T(8,128)(2,1)} %qkvg_hbm.1, ...), custom_call_target="tpu_custom_call" | custom-call | tf_op jit(solution)/shard_map/pallas_call | solution.py:588
  66.8 0.7 %copy.10 = bf16[64,16,128]{2,1,0:T(8,128)(2,1)} copy(bf16[64,16,128]{2,1,0:T(8,128)(2,1)S(1)} %shard_map.82) | data formatting | bytes 524288

commit v5 on v4

v5 whole, which is shorter than its diff:
```python
import math

import jax
import jax.numpy as jnp
from jax import lax
from jax.experimental import pallas as pl
from jax.experimental.pallas import tpu as pltpu
from jax.sharding import PartitionSpec as P

EPS = 1e-05
MESH = pl.DeviceIdType.MESH
F32 = jnp.float32
BF16 = jnp.bfloat16
NT = (((1,), (1,)), ((), ()))
FAR4 = (2, 3, 1, 0)
FAR8 = (4, 5, 7, 3, 6, 2, 1, 0)


def loop(low, high, body, unroll=None):
    def step(index, carry):
        body(index)
        return carry

    lax.fori_loop(low, high, step, 0, unroll=unroll)


def norm_over(values, axis):
    centre = values - jnp.mean(values, axis=axis, keepdims=True)
    spread = jnp.mean(centre * centre, axis=axis, keepdims=True)
    return centre * lax.rsqrt(spread + EPS)


def dot(a, b):
    return jnp.dot(a, b, preferred_element_type=F32)


def dot_nt(a, b):
    return lax.dot_general(a, b, NT, preferred_element_type=F32)


def flip(values):
    return values.astype(F32).T.astype(BF16)


def wait_bytes(ref, sem):
    pltpu.make_async_copy(ref, ref, sem).wait()


def kernel(
    pair_hbm, mask_hbm, mask_rows_hbm, proj_hbm, gate_hbm, tout_hbm, qkvg_hbm, abias_hbm, aout_hbm,
    out_ref,
    pair_ref, mask_smem, mask_ref, proj_ref, gate_ref, tout_ref, qkvg_ref, abias_ref, aout_ref, loads,
    pr_buf, xn, nk, wpt, ms, sb, pt, gt, gate_t, tout_t, qkvg_t,
    a_buf, lt, tr, s_buf, t_buf, tf, updt, n2t, bscr, bm, up,
    x_buf, bias, kt, ve, qe, gq, bf, gs, h_buf,
    send1, recv1, fsend, frecv, send2, recv2, gsend, grecv, psend, precv, xsend, xrecv,
    bsend, bz, bu, send4, recv4,
):
    r = lax.axis_index("row")
    c = lax.axis_index("col")
    q = c >> 1
    p = c & 1
    chip = r * 16 + q
    half = r >> 2
    y = r & 3
    x = c >> 3
    zh = q & 3
    sibling = (r, c ^ 1)

    fetches = [
        pltpu.make_async_copy(source, target, loads.at[at])
        for at, (source, target) in enumerate(
            [
                (pair_hbm, pair_ref), (mask_hbm, mask_smem), (mask_rows_hbm, mask_ref),
                (proj_hbm, proj_ref), (gate_hbm, gate_ref), (tout_hbm, tout_ref),
                (qkvg_hbm, qkvg_ref), (abias_hbm, abias_ref), (aout_hbm, aout_ref),
            ]
        )
    ]
    for fetch in fetches:
        fetch.start()

    barrier = pltpu.get_barrier_semaphore()

    def greet(row, col):
        pl.semaphore_signal(barrier, inc=1, device_id=(row, col), device_id_type=MESH)

    for dz in FAR8:
        for dy in FAR4:
            for dx in FAR4:
                if dz or dy or dx:
                    greet(r ^ ((dz & 1) << 2 | dy), c ^ (dx << 3 | (dz >> 1) << 1))
    for dq in range(16):
        greet(r, c ^ (2 * dq + 1))
    for dz in range(4):
        greet(r ^ 4, c ^ (2 * dz + 1))

    lane = lax.broadcasted_iota(jnp.int32, (1, 128), 1)
    low = lane < 64

    def half_lanes(a, b):
        return jnp.where(low, a, b)

    def swap(values):
        return pltpu.roll(values, 64, 1)

    for fetch in fetches:
        fetch.wait()

    flat = pair_ref[...].astype(F32).reshape(1024, 128)
    xn[...] = norm_over(flat, 1).astype(BF16).astype(F32)
    wpt[...] = flip(proj_ref[...])
    for k in range(16):
        part = xn[pl.ds(k, 64, stride=16), :].astype(BF16)
        nk[k] = jnp.concatenate([part, part], axis=0)

    two = mask_ref[pl.ds(r >> 1, 1), :].astype(F32)
    odd = (r & 1) == 1
    turned = swap(jnp.broadcast_to(two, (8, 128)))[0:1]
    is_left = (lane >> 6) == jnp.where(odd, 0, 1)
    row_live = half_lanes(jnp.where(odd, turned, two), jnp.where(odd, two, turned))
    col_live = [mask_smem[c * 16 + k].astype(F32) for k in range(16)]

    pl.semaphore_wait(barrier, 147)

    def project(step):
        to_y = y ^ 2 ^ step ^ (step >> 1)
        first = pl.multiple_of(to_y * 16, 16)
        weights = jnp.concatenate(
            [wpt[pl.ds(64 * b + first, 16), :] for b in range(8)], axis=0
        )
        for k in range(16):
            z = dot_nt(weights, nk[k])
            g = jnp.where(is_left, z[0:32], z[64:96])
            v = jnp.where(is_left, z[32:64], z[96:128])
            ms[pl.ds(k, 32, stride=16), :] = jax.nn.sigmoid(g) * v * (row_live * col_live[k])
        for zl in range(2):
            sb[zl, to_y] = ms[256 * zl : 256 * zl + 256, :].astype(BF16).reshape(16, 16, 128)

        def send(dx, dz):
            to_zl = half ^ (dz & 1)
            flips = dx << 2 | dz >> 1
            return pltpu.make_async_remote_copy(
                src_ref=sb.at[to_zl, to_y, q ^ flips],
                dst_ref=a_buf.at[p, r, q],
                send_sem=send1,
                recv_sem=recv1.at[r],
                device_id=(to_zl * 4 + to_y, c ^ (flips << 1)),
                device_id_type=MESH,
            )

        for dx in FAR4:
            for dz in FAR8:
                if dx or dz:
                    send(dx, dz).start()

        @pl.when(step < 3)
        def _():
            send(0, 0).start()

        @pl.when(step == 3)
        def _():
            pltpu.make_async_copy(sb.at[half, y, q], a_buf.at[p, r, q], recv1.at[r]).start()

    loop(0, 4, project)
    sent = [lambda: wait_bytes(sb.at[0], send1), lambda: wait_bytes(sb.at[0, pl.ds(0, 3)], send1)]
    sent.append(lambda: wait_bytes(sb.at[0, 0, pl.ds(0, 15)], send1))

    def pair_send(flips):
        to = c ^ flips
        pltpu.make_async_remote_copy(
            src_ref=pair_ref.at[pl.ds(2 * to, 2)],
            dst_ref=pr_buf.at[:, c],
            send_sem=psend,
            recv_sem=precv,
            device_id=(r, to),
            device_id_type=MESH,
        ).start()

    for dx in FAR4:
        for dz in FAR4:
            for core in range(2):
                if dx or dz or core:
                    pair_send(dx << 3 | dz << 1 | core)
    pltpu.make_async_copy(pair_ref.at[pl.ds(2 * c, 2)], pr_buf.at[:, c], precv).start()
    sent.append(lambda: wait_bytes(pr_buf.at[:, pl.ds(0, 31)], psend))

    gate_t[...] = flip(gate_ref[...])
    tout_t[...] = flip(tout_ref[...])
    qkvg_t[...] = flip(qkvg_ref[...])

    def forward_copy(row):
        return pltpu.make_async_remote_copy(
            src_ref=a_buf.at[p, row],
            dst_ref=a_buf.at[p, row],
            send_sem=fsend.at[row],
            recv_sem=frecv.at[row],
            device_id=sibling,
            device_id_type=MESH,
        )

    def turn(core, row):
        @pl.when((row >> 2) == p)
        def _():
            part = flip(a_buf[core, row].reshape(256, 128))
            at = pl.multiple_of((row & 3) * 64, 64)
            lt[core, pl.ds(at, 64), :] = jnp.where((row & 1) == 1, part[0:64], part[64:128])

    def arriving(step):
        pair = step >> 1
        return r ^ (2 ^ pair ^ (pair >> 1)) ^ ((step & 1) << 2)

    def forward(step):
        row = arriving(step)
        wait_bytes(a_buf.at[p, row], recv1.at[row])
        forward_copy(row).start()
        turn(p, row)

    loop(0, 8, forward)
    sent.append(lambda: loop(0, 8, lambda row: forward_copy(row).wait_send()))

    def turn_other(step):
        row = arriving(step)
        wait_bytes(a_buf.at[1 - p, row], frecv.at[row])
        turn(1 - p, row)

    loop(0, 8, turn_other, unroll=4)

    def triangle(step):
        pair = (y >> 1) ^ 1 ^ step
        rows = pl.ds(pl.multiple_of(128 * pair, 128), 128)
        for jc in range(4):
            sides = [
                jnp.concatenate(
                    [a_buf[core, 2 * jc + e].reshape(256, 128) for e in range(2)], axis=1
                )
                for core in range(2)
            ]
            prod = dot(lt[0, rows, :], sides[0]) + dot(lt[1, rows, :], sides[1])
            tr[pl.ds(jc, 128, stride=4), :] = half_lanes(prod[:, 0:128], prod[:, 128:256])
        for e in range(2):
            s_buf[2 * pair + e] = tr[256 * e : 256 * e + 256, :].astype(BF16).reshape(16, 16, 128)

        def send(to_y, flips):
            return pltpu.make_async_remote_copy(
                src_ref=s_buf.at[to_y, q ^ flips],
                dst_ref=t_buf.at[chip],
                send_sem=send2,
                recv_sem=recv2.at[r],
                device_id=(4 * p + to_y, c ^ (flips << 1)),
                device_id_type=MESH,
            )

        for own in range(2):
            to_y = y ^ (2 * (1 - step)) ^ (own ^ step)
            for dx in FAR4:
                for dz in FAR4:
                    if dx or dz:
                        send(to_y, dx << 2 | dz).start()
            here = jnp.logical_and(to_y == y, p == half)

            @pl.when(jnp.logical_not(here))
            def _():
                send(to_y, 0).start()

            @pl.when(here)
            def _():
                pltpu.make_async_copy(s_buf.at[to_y, q], t_buf.at[chip], recv2.at[r]).start()

    loop(0, 2, triangle, unroll=2)

    def triangle_sent():
        wait_bytes(s_buf.at[pl.ds(0, 3)], send2)
        wait_bytes(s_buf.at[0, pl.ds(0, 15)], send2)

        @pl.when(p != half)
        def _():
            wait_bytes(s_buf.at[0, 0], send2)

    sent.append(triangle_sent)

    wait_bytes(pr_buf, precv)

    def prepare(s):
        at = s & 3
        rows = pr_buf[s >> 2, pl.ds(8 * at, 8)].astype(F32).reshape(128, 128)
        pt[s] = rows.T
        gt[s] = jax.nn.sigmoid(dot_nt(gate_t[...], norm_over(rows, 1).astype(BF16)))

    loop(0, 8, prepare, unroll=2)

    def hand_copy(row):
        block = t_buf.at[pl.ds(pl.multiple_of(row * 16, 16), 16)]
        return pltpu.make_async_remote_copy(
            src_ref=block,
            dst_ref=block,
            send_sem=gsend.at[row],
            recv_sem=grecv.at[row],
            device_id=sibling,
            device_id_type=MESH,
        )

    def widen(row):
        block = t_buf[pl.ds(pl.multiple_of(row * 16, 16), 16)]
        tf[pl.ds(pl.multiple_of(row * 256, 256), 256), :] = block.astype(F32).reshape(256, 128)

    @pl.when(p == half)
    def _():
        def hand(step):
            row = arriving(step)
            wait_bytes(t_buf.at[pl.ds(pl.multiple_of(row * 16, 16), 16)], recv2.at[row])
            hand_copy(row).start()
            widen(row)

        loop(0, 8, hand, unroll=4)

    @pl.when(p != half)
    def _():
        def take(step):
            row = arriving(step)
            wait_bytes(t_buf.at[pl.ds(pl.multiple_of(row * 16, 16), 16)], grecv.at[row])
            widen(row)

        loop(0, 8, take, unroll=4)

    def handed():
        @pl.when(p == half)
        def _():
            loop(0, 8, lambda row: hand_copy(row).wait_send())

    sent.append(handed)

    def home(s):
        tri = tf[pl.ds(8 * p + s, 128, stride=16), :]
        tri_norm = norm_over(tri, 0).astype(BF16)
        updated = pt[s] + gt[s] * dot(tout_t[...], tri_norm)
        updt[s] = updated
        norm_two = norm_over(updated, 0)
        n2t[s] = norm_two
        heads = dot(abias_ref[...], norm_two.astype(BF16))[0:4]
        live = mask_ref[pl.ds(s & 3, 1), :] > 0
        bscr[s & 1, pl.ds(8 * ((s & 3) >> 1) + (s >> 2), 4, stride=2), :] = jnp.where(
            live, heads, -1000000000.0
        )

    loop(0, 8, home, unroll=4)

    bm[:, 0:128] = bscr[0].astype(BF16)
    bm[:, 128:256] = bscr[1].astype(BF16)

    def bias_copy(src, dst, sem, recv, row, col):
        return pltpu.make_async_remote_copy(
            src_ref=src, dst_ref=dst, send_sem=bsend.at[sem], recv_sem=recv,
            device_id=(row, col), device_id_type=MESH,
        )

    def along_z(dz):
        to = (c ^ ((dz >> 1) << 1)) & 30 | half
        return bias_copy(bm, bias.at[p, y, x, zh], 0, bz, r ^ ((dz & 1) << 2), to)

    for dz in FAR8:
        if dz:
            along_z(dz).start()

    @pl.when(p == half)
    def _():
        pltpu.make_async_copy(bm, bias.at[p, y, x, zh], bz).start()

    @pl.when(p != half)
    def _():
        along_z(0).start()

    def bias_z_sent():
        wait_bytes(bias.at[0, 0, 0], bsend.at[0])
        wait_bytes(bias.at[0, 0, 0, pl.ds(0, 3)], bsend.at[0])

        @pl.when(p != half)
        def _():
            wait_bytes(bias.at[0, 0, 0, 0], bsend.at[0])

    sent.append(bias_z_sent)

    def rows_of(s):
        at = pl.ds(pl.multiple_of(128 * (s & 3), 128), 128)
        x_buf[2 * p + (s >> 2), at, :] = n2t[s].T.astype(BF16)
        up[2 * p + (s >> 2), at, :] = updt[s].T

    loop(0, 8, rows_of, unroll=4)

    def to_sibling(ref, at):
        return pltpu.make_async_remote_copy(
            src_ref=ref, dst_ref=ref, send_sem=xsend.at[at], recv_sem=xrecv.at[at],
            device_id=sibling, device_id_type=MESH,
        )

    swaps = [
        to_sibling(x_buf.at[pl.ds(2 * p, 2)], 0),
        to_sibling(up.at[pl.ds(2 * p, 2), pl.ds(pl.multiple_of(256 * (1 - p), 256), 256)], 1),
    ]
    for swapping in swaps:
        swapping.start()
        sent.append(swapping.wait_send)

    def unit_copy(core, unit_y, unit_x, dy, dx):
        unit = bias.at[core, unit_y, unit_x]
        return bias_copy(unit, unit, 1, bu.at[core, unit_y, unit_x], r ^ dy, c ^ (dx << 3))

    def unit_wait(core, unit_y, unit_x):
        wait_bytes(bias.at[core, unit_y, unit_x], bu.at[core, unit_y, unit_x])

    wait_bytes(bias.at[:, 0, 0], bz)
    for d in (1, 3, 2):
        unit_copy(0, y, x, 0, d).start()
        unit_copy(1, y, x, 0, d).start()
    for d in (1, 3, 2):
        unit_copy(0, y, x, d, 0).start()
        unit_copy(1, y, x, d, 0).start()
    row_at = lax.broadcasted_iota(jnp.int32, (256, 64), 0)
    spread = ((row_at // 8) * 2 + row_at % 2 == lax.broadcasted_iota(jnp.int32, (256, 64), 1)).astype(
        F32
    ).astype(BF16)
    lane_at = lax.broadcasted_iota(jnp.int32, (64, 256), 1)
    gather = ((lane_at // 8) * 2 + lane_at % 2 == lax.broadcasted_iota(jnp.int32, (64, 256), 0)).astype(
        F32
    ).astype(BF16)
    own_head = (lax.broadcasted_iota(jnp.int32, (256, 128), 0) % 8) // 2 == (
        lax.broadcasted_iota(jnp.int32, (256, 128), 1) // 32
    )

    def project_row(i):
        rows = x_buf[i]
        kt[i] = dot_nt(qkvg_t[128:256, :], rows).astype(BF16)
        ve[i, :, 0:128] = dot(rows, qkvg_ref[:, 256:384]).astype(BF16)
        ve[i, :, 128:256] = jnp.ones((512, 128), BF16)
        mine = x_buf[i, pl.ds(pl.multiple_of(256 * p, 256), 256), :]
        queries = dot(mine, qkvg_ref[:, 0:128]).astype(BF16)
        gq[i] = jax.nn.sigmoid(dot(mine, qkvg_ref[:, 384:512]))
        for unit_y in range(4):
            wide = dot(spread, queries[64 * unit_y : 64 * unit_y + 64])
            qe[i, unit_y] = jnp.where(own_head, wide, 0.0).astype(BF16)

    for own in range(2):
        project_row(2 * p + own)

    for near in (1, 3, 2):
        unit_wait(0, y, x ^ near)
    for dy in (1, 3, 2):
        for near in (1, 3, 2):
            unit_copy(0, y, x ^ near, dy, 0).start()
        unit_wait(1, y ^ dy, x)
        for dx in (1, 3, 2):
            unit_copy(1, y ^ dy, x, 0, dx).start()

    def bias_sent():
        wait_bytes(bias.at[0], bsend.at[1])
        wait_bytes(bias.at[1, pl.ds(0, 3)], bsend.at[1])
        wait_bytes(bias.at[1, 0, pl.ds(0, 2)], bsend.at[1])

    sent.append(bias_sent)

    for swapping in swaps:
        swapping.wait_recv()
    for own in range(2):
        project_row(2 - 2 * p + own)

    log2e = 1.0 / math.log(2.0)
    scale = log2e / math.sqrt(32.0)

    def attend(i, unit_y):
        scores = dot(qe[i, unit_y], kt[i]) * scale + bf[...].reshape(256, 512)
        exps = jnp.exp2(scores - jnp.max(scores, axis=1, keepdims=True)).astype(BF16)
        out = dot(exps, ve[i])
        out = jnp.where(own_head, out[:, 0:128] * (1.0 / out[:, 128:256]), 0.0)
        high = out.astype(BF16)
        rest = (out - high.astype(F32)).astype(BF16)
        attended = dot(gather, high) + dot(gather, rest)
        at = pl.multiple_of(64 * unit_y, 64)
        gated = (gq[i, pl.ds(at, 64), :] * attended).astype(BF16)
        result = up[i, pl.ds(pl.multiple_of(256 * p + at, 64), 64), :] + dot(gated, aout_ref[...])
        gs[i, pl.ds(4 * unit_y, 4)] = result.astype(BF16).reshape(4, 16, 128)

    def block(step):
        unit_y = y ^ step ^ (step >> 1)

        @pl.when(step == 0)
        def _():
            for d in (1, 3, 2):
                unit_wait(1, y, x ^ d)

        @pl.when(step > 0)
        def _():
            unit_wait(0, unit_y, x)
            for d in (1, 3, 2):
                unit_wait(0, unit_y, x ^ d)
                unit_wait(1, unit_y, x ^ d)

        for core in range(2):
            tiles = bias[core, unit_y].reshape(16, 16, 256).astype(F32) * log2e
            bf[:, core, :, 0:256] = tiles[:, 0:8]
            bf[:, core, :, 256:512] = tiles[:, 8:16]
        for i in range(4):
            attend(i, unit_y)

        for off in range(4):
            cl = 4 * unit_y + off
            send_gated(cl)

    def send_gated(cl):
        to = 16 * p + cl

        @pl.when(to == c)
        def _():
            pltpu.make_async_copy(gs.at[:, cl], h_buf.at[pl.ds(4 * q, 4)], recv4).start()

        @pl.when(to != c)
        def _():
            pltpu.make_async_remote_copy(
                src_ref=gs.at[:, cl],
                dst_ref=h_buf.at[pl.ds(4 * q, 4)],
                send_sem=send4,
                recv_sem=recv4,
                device_id=(r, to),
                device_id_type=MESH,
            ).start()

    loop(0, 4, block)

    def gated_sent():
        wait_bytes(gs.at[:, pl.ds(0, 15)], send4)

        @pl.when((c >> 4) != p)
        def _():
            wait_bytes(gs.at[:, 0], send4)

    sent.append(gated_sent)

    for wait in sent:
        wait()

    wait_bytes(h_buf, recv4)
    out_ref[...] = h_buf[...]


def local(pair_map, res_mask, tri_proj, tri_gate, tri_out, att_qkvg, att_bias, att_out):
    dma = pltpu.SemaphoreType.DMA
    return pl.pallas_call(
        kernel,
        out_shape=jax.ShapeDtypeStruct((64, 16, 128), BF16),
        in_specs=[pl.BlockSpec(memory_space=pltpu.HBM)] * 9,
        out_specs=pl.BlockSpec(memory_space=pltpu.VMEM),
        scratch_shapes=[
            pltpu.VMEM((64, 16, 128), BF16),
            pltpu.SMEM((512,), jnp.int32),
            pltpu.VMEM((4, 128), jnp.int32),
            pltpu.VMEM((128, 512), BF16),
            pltpu.VMEM((128, 128), BF16),
            pltpu.VMEM((128, 128), BF16),
            pltpu.VMEM((128, 512), BF16),
            pltpu.VMEM((4, 128), BF16),
            pltpu.VMEM((128, 128), BF16),
            dma((9,)),
            pltpu.VMEM((2, 32, 16, 128), BF16),
            pltpu.VMEM((1024, 128), F32),
            pltpu.VMEM((16, 128, 128), BF16),
            pltpu.VMEM((512, 128), BF16),
            pltpu.VMEM((512, 128), F32),
            pltpu.VMEM((2, 4, 16, 16, 128), BF16),
            pltpu.VMEM((8, 128, 128), F32),
            pltpu.VMEM((8, 128, 128), F32),
            pltpu.VMEM((128, 128), BF16),
            pltpu.VMEM((128, 128), BF16),
            pltpu.VMEM((512, 128), BF16),
            pltpu.VMEM((2, 8, 16, 16, 128), BF16),
            pltpu.VMEM((2, 256, 256), BF16),
            pltpu.VMEM((512, 128), F32),
            pltpu.VMEM((4, 16, 16, 128), BF16),
            pltpu.VMEM((128, 16, 128), BF16),
            pltpu.VMEM((2048, 128), F32),
            pltpu.VMEM((8, 128, 128), F32),
            pltpu.VMEM((8, 128, 128), F32),
            pltpu.VMEM((2, 16, 128), F32),
            pltpu.VMEM((16, 256), BF16),
            pltpu.VMEM((4, 512, 128), F32),
            pltpu.VMEM((4, 512, 128), BF16),
            pltpu.VMEM((2, 4, 4, 4, 16, 256), BF16),
            pltpu.VMEM((4, 128, 512), BF16),
            pltpu.VMEM((4, 512, 256), BF16),
            pltpu.VMEM((4, 4, 256, 128), BF16),
            pltpu.VMEM((4, 256, 128), F32),
            pltpu.VMEM((16, 2, 8, 512), F32),
            pltpu.VMEM((4, 16, 16, 128), BF16),
            pltpu.VMEM((64, 16, 128), BF16),
            dma, dma((8,)),
            dma((8,)), dma((8,)),
            dma, dma((8,)),
            dma((8,)), dma((8,)),
            dma, dma,
            dma((2,)), dma((2,)),
            dma((2,)),
            dma, dma((2, 4, 4)),
            dma, dma,
        ],
        compiler_params=pltpu.CompilerParams(
            collective_id=0, has_side_effects=True, vmem_limit_bytes=48 * 1024 * 1024
        ),
    )(
        *(
            pltpu.with_memory_space_constraint(operand, pltpu.HBM)
            for operand in (
                pair_map, res_mask, res_mask.reshape(4, 128), tri_proj, tri_gate, tri_out, att_qkvg,
                att_bias.T, att_out,
            )
        )
    )


def solution(mesh):
    in_specs = (P("row", "col", None), P(), P(), P(), P(), P(), P(), P())
    out_specs = P("row", "col", None)
    return jax.shard_map(local, mesh=mesh, in_specs=in_specs, out_specs=out_specs, check_vma=False)
```

time: 67.6 us -> 70.3 us (1.040)
  Pallas kernels: 66.8 us -> 69.4 us
    pallas_call x1, Pallas kernels: 66.8 us -> 69.4 us  [local(): pl.pallas_call(kernel, out_shape=jax.ShapeDtypeStruct((64, 16, 128), BF16...]
where the time goes in v5:
time: 70.3 us; the launch traced here: 70.2 us
  Pallas kernels  69.4 us (99%)
  local copies, waits for them, and re-layouts  0.71 us (1%)
    pallas_call x1, Pallas kernels, local(): pl.pallas_call(kernel, out_shape=jax.ShapeDtypeStruct((64, 16, 128), BF16...  69.4 us

profile of v5, /device:TPU:3, one launch (start us, length us, event | category | flops | bytes accessed | tf_op | source)
XLA Modules:
  0.0 70.2 jit_solution(12349377319959674141)
XLA Ops:
  0.0 69.4 %shard_map.82 = bf16[64,16,128]{2,1,0:T(8,128)(2,1)S(1)} custom-call(bf16[64,16,128]{2,1,0:T(8,128)(2,1)} %pair_hbm.1, s32[512]{0:T(512)} %mask_hbm.1, s32[4,128]{1,0:T(4,128)} %bitcast.2, bf16[128,512]{1,0:T(8,128)(2,1)} %proj_hbm.1, bf16[128,128]{1,0:T(8,128)(2,1)} %gate_hbm.1, bf16[128,128]{1,0:T(8,128)(2,1)} %tout_hbm.1, bf16[128,512]{1,0:T(8,128)(2,1)} %qkvg_hbm.1, ...), custom_call_target="tpu_custom_call" | custom-call | tf_op jit(solution)/shard_map/pallas_call | solution.py:546
  69.5 0.7 %copy.10 = bf16[64,16,128]{2,1,0:T(8,128)(2,1)} copy(bf16[64,16,128]{2,1,0:T(8,128)(2,1)S(1)} %shard_map.82) | data formatting | bytes 524288

commit v6 on v5

--- a/solution.py
+++ b/solution.py
@@ -12,6 +12,7 @@
 F32 = jnp.float32
 BF16 = jnp.bfloat16
 NT = (((1,), (1,)), ((), ()))
+ROWS = 4
 FAR4 = (2, 3, 1, 0)
 FAR8 = (4, 5, 7, 3, 6, 2, 1, 0)
 
@@ -52,7 +53,7 @@
     pair_ref, mask_smem, mask_ref, proj_ref, gate_ref, tout_ref, qkvg_ref, abias_ref, aout_ref, loads,
     pr_buf, xn, nk, wpt, ms, sb, pt, gt, gate_t, tout_t, qkvg_t,
     a_buf, lt, tr, s_buf, t_buf, tf, updt, n2t, bscr, bm, up,
-    x_buf, bias, kt, ve, qe, gq, bf, gs, h_buf,
+    x_buf, bias, kt, ve, qe, gq, bf, sc, wb, mixed, gs, h_buf,
     send1, recv1, fsend, frecv, send2, recv2, gsend, grecv, psend, precv, xsend, xrecv,
     bsend, bz, bu, send4, recv4,
 ):
@@ -121,9 +122,8 @@
     row_live = half_lanes(jnp.where(odd, turned, two), jnp.where(odd, two, turned))
     col_live = [mask_smem[c * 16 + k].astype(F32) for k in range(16)]
 
-    pl.semaphore_wait(barrier, 147)
-
-    def project(step):
+
+    def tiles(step):
         to_y = y ^ 2 ^ step ^ (step >> 1)
         first = pl.multiple_of(to_y * 16, 16)
         weights = jnp.concatenate(
@@ -136,6 +136,9 @@
             ms[pl.ds(k, 32, stride=16), :] = jax.nn.sigmoid(g) * v * (row_live * col_live[k])
         for zl in range(2):
             sb[zl, to_y] = ms[256 * zl : 256 * zl + 256, :].astype(BF16).reshape(16, 16, 128)
+
+    def project(step):
+        to_y = y ^ 2 ^ step ^ (step >> 1)
 
         def send(dx, dz):
             to_zl = half ^ (dz & 1)
@@ -162,7 +165,15 @@
         def _():
             pltpu.make_async_copy(sb.at[half, y, q], a_buf.at[p, r, q], recv1.at[r]).start()
 
-    loop(0, 4, project)
+    tiles(0)
+    pl.semaphore_wait(barrier, 147)
+    project(0)
+
+    def rest(step):
+        tiles(step)
+        project(step)
+
+    loop(1, 4, rest)
     sent = [lambda: wait_bytes(sb.at[0], send1), lambda: wait_bytes(sb.at[0, pl.ds(0, 3)], send1)]
     sent.append(lambda: wait_bytes(sb.at[0, 0, pl.ds(0, 15)], send1))
 
@@ -356,7 +367,7 @@
 
     def along_z(dz):
         to = (c ^ ((dz >> 1) << 1)) & 30 | half
-        return bias_copy(bm, bias.at[p, y, x, zh], 0, bz, r ^ ((dz & 1) << 2), to)
+        return bias_copy(bm, bias.at[p, y, x, zh], 0, bz.at[zh], r ^ ((dz & 1) << 2), to)
 
     for dz in FAR8:
         if dz:
@@ -364,7 +375,7 @@
 
     @pl.when(p == half)
     def _():
-        pltpu.make_async_copy(bm, bias.at[p, y, x, zh], bz).start()
+        pltpu.make_async_copy(bm, bias.at[p, y, x, zh], bz.at[zh]).start()
 
     @pl.when(p != half)
     def _():
@@ -408,13 +419,18 @@
     def unit_wait(core, unit_y, unit_x):
         wait_bytes(bias.at[core, unit_y, unit_x], bu.at[core, unit_y, unit_x])
 
-    wait_bytes(bias.at[:, 0, 0], bz)
-    for d in (1, 3, 2):
-        unit_copy(0, y, x, 0, d).start()
-        unit_copy(1, y, x, 0, d).start()
-    for d in (1, 3, 2):
-        unit_copy(0, y, x, d, 0).start()
-        unit_copy(1, y, x, d, 0).start()
+    def part_copy(core, part, dy, dx):
+        block = bias.at[core, y, x, part]
+        return bias_copy(block, block, 1, bu.at[core, y, x], r ^ dy, c ^ (dx << 3))
+
+    for flips in (0, 1, 3, 2):
+        part = zh ^ flips
+        wait_bytes(bias.at[:, 0, 0, 0], bz.at[part])
+        for d in (1, 3, 2):
+            for core in range(2):
+                part_copy(core, part, 0, d).start()
+                part_copy(core, part, d, 0).start()
+
     row_at = lax.broadcasted_iota(jnp.int32, (256, 64), 0)
     spread = ((row_at // 8) * 2 + row_at % 2 == lax.broadcasted_iota(jnp.int32, (256, 64), 1)).astype(
         F32
@@ -439,6 +455,13 @@
             wide = dot(spread, queries[64 * unit_y : 64 * unit_y + 64])
             qe[i, unit_y] = jnp.where(own_head, wide, 0.0).astype(BF16)
 
+    log2e = 1.0 / math.log(2.0)
+    scale = log2e / math.sqrt(32.0)
+
+    def scores_of(i):
+        for unit_y in range(4):
+            sc[unit_y, i] = dot(qe[i, unit_y], kt[i]) * scale
+
     for own in range(2):
         project_row(2 * p + own)
 
@@ -461,23 +484,25 @@
     for swapping in swaps:
         swapping.wait_recv()
     for own in range(2):
+        scores_of(2 * p + own)
+    for own in range(2):
         project_row(2 - 2 * p + own)
-
-    log2e = 1.0 / math.log(2.0)
-    scale = log2e / math.sqrt(32.0)
-
-    def attend(i, unit_y):
-        scores = dot(qe[i, unit_y], kt[i]) * scale + bf[...].reshape(256, 512)
-        exps = jnp.exp2(scores - jnp.max(scores, axis=1, keepdims=True)).astype(BF16)
-        out = dot(exps, ve[i])
+    for own in range(2):
+        scores_of(2 - 2 * p + own)
+
+    def soften(i, unit_y):
+        for at in range(0, 16, ROWS):
+            part = sc[unit_y, i, 16 * at : 16 * (at + ROWS), :]
+            part = part + bf[at : at + ROWS].reshape(16 * ROWS, 512)
+            exps = jnp.exp2(part - jnp.max(part, axis=1, keepdims=True))
+            wb[i, 16 * at : 16 * (at + ROWS), :] = exps.astype(BF16)
+
+    def mix(i):
+        out = dot(wb[i], ve[i])
         out = jnp.where(own_head, out[:, 0:128] * (1.0 / out[:, 128:256]), 0.0)
         high = out.astype(BF16)
-        rest = (out - high.astype(F32)).astype(BF16)
-        attended = dot(gather, high) + dot(gather, rest)
-        at = pl.multiple_of(64 * unit_y, 64)
-        gated = (gq[i, pl.ds(at, 64), :] * attended).astype(BF16)
-        result = up[i, pl.ds(pl.multiple_of(256 * p + at, 64), 64), :] + dot(gated, aout_ref[...])
-        gs[i, pl.ds(4 * unit_y, 4)] = result.astype(BF16).reshape(4, 16, 128)
+        mixed[0, :, 128 * i : 128 * i + 128] = high
+        mixed[1, :, 128 * i : 128 * i + 128] = (out - high.astype(F32)).astype(BF16)
 
     def block(step):
         unit_y = y ^ step ^ (step >> 1)
@@ -499,7 +524,20 @@
             bf[:, core, :, 0:256] = tiles[:, 0:8]
             bf[:, core, :, 256:512] = tiles[:, 8:16]
         for i in range(4):
-            attend(i, unit_y)
+            soften(i, unit_y)
+            if i > 0:
+                mix(i - 1)
+        mix(3)
+        attended = dot(gather, mixed[0]) + dot(gather, mixed[1])
+        at = pl.multiple_of(64 * unit_y, 64)
+        gated = jnp.concatenate(
+            [gq[i, pl.ds(at, 64), :] * attended[:, 128 * i : 128 * i + 128] for i in range(4)], axis=0
+        )
+        update = dot(gated.astype(BF16), aout_ref[...])
+        for i in range(4):
+            result = up[i, pl.ds(pl.multiple_of(256 * p + at, 64), 64), :]
+            result = result + update[64 * i : 64 * i + 64]
+            gs[i, pl.ds(4 * unit_y, 4)] = result.astype(BF16).reshape(4, 16, 128)
 
         for off in range(4):
             cl = 4 * unit_y + off
@@ -588,6 +626,9 @@
             pltpu.VMEM((4, 4, 256, 128), BF16),
             pltpu.VMEM((4, 256, 128), F32),
             pltpu.VMEM((16, 2, 8, 512), F32),
+            pltpu.VMEM((4, 4, 256, 512), F32),
+            pltpu.VMEM((4, 256, 512), BF16),
+            pltpu.VMEM((2, 256, 512), BF16),
             pltpu.VMEM((4, 16, 16, 128), BF16),
             pltpu.VMEM((64, 16, 128), BF16),
             dma, dma((8,)),
@@ -597,7 +638,7 @@
             dma, dma,
             dma((2,)), dma((2,)),
             dma((2,)),
-            dma, dma((2, 4, 4)),
+            dma((4,)), dma((2, 4, 4)),
             dma, dma,
         ],
         compiler_params=pltpu.CompilerParams(

time: 70.3 us -> 65.1 us (0.926)
  Pallas kernels: 69.4 us -> 64.3 us
    pallas_call x1, Pallas kernels: 69.4 us -> 64.3 us  [local(): pl.pallas_call(kernel, out_shape=jax.ShapeDtypeStruct((64, 16, 128), BF16...]
where the time goes in v6:
time: 65.1 us; the launch traced here: 65 us
  Pallas kernels  64.3 us (99%)
  local copies, waits for them, and re-layouts  0.71 us (1%)
    pallas_call x1, Pallas kernels, local(): pl.pallas_call(kernel, out_shape=jax.ShapeDtypeStruct((64, 16, 128), BF16...  64.3 us

profile of v6, /device:TPU:3, one launch (start us, length us, event | category | flops | bytes accessed | tf_op | source)
XLA Modules:
  0.0 65.0 jit_solution(6566137024986068288)
XLA Ops:
  0.0 64.3 %shard_map.82 = bf16[64,16,128]{2,1,0:T(8,128)(2,1)S(1)} custom-call(bf16[64,16,128]{2,1,0:T(8,128)(2,1)} %pair_hbm.1, s32[512]{0:T(512)} %mask_hbm.1, s32[4,128]{1,0:T(4,128)} %bitcast.2, bf16[128,512]{1,0:T(8,128)(2,1)} %proj_hbm.1, bf16[128,128]{1,0:T(8,128)(2,1)} %gate_hbm.1, bf16[128,128]{1,0:T(8,128)(2,1)} %tout_hbm.1, bf16[128,512]{1,0:T(8,128)(2,1)} %qkvg_hbm.1, ...), custom_call_target="tpu_custom_call" | custom-call | tf_op jit(solution)/shard_map/pallas_call | solution.py:584
  64.3 0.7 %copy.10 = bf16[64,16,128]{2,1,0:T(8,128)(2,1)} copy(bf16[64,16,128]{2,1,0:T(8,128)(2,1)S(1)} %shard_map.82) | data formatting | bytes 524288

commit v7 on v6

--- a/solution.py
+++ b/solution.py
@@ -12,7 +12,6 @@
 F32 = jnp.float32
 BF16 = jnp.bfloat16
 NT = (((1,), (1,)), ((), ()))
-ROWS = 4
 FAR4 = (2, 3, 1, 0)
 FAR8 = (4, 5, 7, 3, 6, 2, 1, 0)
 
@@ -354,7 +353,7 @@
             live, heads, -1000000000.0
         )
 
-    loop(0, 8, home, unroll=4)
+    loop(0, 8, home, unroll=8)
 
     bm[:, 0:128] = bscr[0].astype(BF16)
     bm[:, 128:256] = bscr[1].astype(BF16)
@@ -367,7 +366,7 @@
 
     def along_z(dz):
         to = (c ^ ((dz >> 1) << 1)) & 30 | half
-        return bias_copy(bm, bias.at[p, y, x, zh], 0, bz.at[zh], r ^ ((dz & 1) << 2), to)
+        return bias_copy(bm, bias.at[p, y, x, zh], 0, bz.at[zh >> 1], r ^ ((dz & 1) << 2), to)
 
     for dz in FAR8:
         if dz:
@@ -375,7 +374,7 @@
 
     @pl.when(p == half)
     def _():
-        pltpu.make_async_copy(bm, bias.at[p, y, x, zh], bz.at[zh]).start()
+        pltpu.make_async_copy(bm, bias.at[p, y, x, zh], bz.at[zh >> 1]).start()
 
     @pl.when(p != half)
     def _():
@@ -412,24 +411,36 @@
         swapping.start()
         sent.append(swapping.wait_send)
 
-    def unit_copy(core, unit_y, unit_x, dy, dx):
-        unit = bias.at[core, unit_y, unit_x]
-        return bias_copy(unit, unit, 1, bu.at[core, unit_y, unit_x], r ^ dy, c ^ (dx << 3))
-
-    def unit_wait(core, unit_y, unit_x):
-        wait_bytes(bias.at[core, unit_y, unit_x], bu.at[core, unit_y, unit_x])
-
-    def part_copy(core, part, dy, dx):
-        block = bias.at[core, y, x, part]
-        return bias_copy(block, block, 1, bu.at[core, y, x], r ^ dy, c ^ (dx << 3))
-
-    for flips in (0, 1, 3, 2):
-        part = zh ^ flips
-        wait_bytes(bias.at[:, 0, 0, 0], bz.at[part])
+    def unit_of(core, unit_y, unit_x, part):
+        return bias.at[core, unit_y, unit_x, pl.ds(2 * part, 2)]
+
+    def unit_copy(core, unit_y, unit_x, part, dy, dx):
+        unit = unit_of(core, unit_y, unit_x, part)
+        return bias_copy(
+            unit, unit, 1, bu.at[core, unit_y, unit_x, part], r ^ dy, c ^ (dx << 3)
+        )
+
+    def unit_wait(core, unit_y, unit_x, part):
+        wait_bytes(unit_of(core, unit_y, unit_x, part), bu.at[core, unit_y, unit_x, part])
+
+    def straight(own):
+        part = (zh >> 1) ^ own
+        wait_bytes(bias.at[:, 0, 0, pl.ds(0, 2)], bz.at[part])
         for d in (1, 3, 2):
             for core in range(2):
-                part_copy(core, part, 0, d).start()
-                part_copy(core, part, d, 0).start()
+                unit_copy(core, y, x, part, 0, d).start()
+                unit_copy(core, y, x, part, d, 0).start()
+
+    def onward(own):
+        part = (zh >> 1) ^ own
+        for near in (1, 3, 2):
+            unit_wait(0, y, x ^ near, part)
+        for dy in (1, 3, 2):
+            for near in (1, 3, 2):
+                unit_copy(0, y, x ^ near, part, dy, 0).start()
+            unit_wait(1, y ^ dy, x, part)
+            for dx in (1, 3, 2):
+                unit_copy(1, y ^ dy, x, part, 0, dx).start()
 
     row_at = lax.broadcasted_iota(jnp.int32, (256, 64), 0)
     spread = ((row_at // 8) * 2 + row_at % 2 == lax.broadcasted_iota(jnp.int32, (256, 64), 1)).astype(
@@ -462,17 +473,14 @@
         for unit_y in range(4):
             sc[unit_y, i] = dot(qe[i, unit_y], kt[i]) * scale
 
-    for own in range(2):
-        project_row(2 * p + own)
-
-    for near in (1, 3, 2):
-        unit_wait(0, y, x ^ near)
-    for dy in (1, 3, 2):
-        for near in (1, 3, 2):
-            unit_copy(0, y, x ^ near, dy, 0).start()
-        unit_wait(1, y ^ dy, x)
-        for dx in (1, 3, 2):
-            unit_copy(1, y ^ dy, x, 0, dx).start()
+    straight(0)
+    project_row(2 * p)
+    straight(1)
+    project_row(2 * p + 1)
+    onward(0)
+    scores_of(2 * p)
+    onward(1)
+    scores_of(2 * p + 1)
 
     def bias_sent():
         wait_bytes(bias.at[0], bsend.at[1])
@@ -484,18 +492,20 @@
     for swapping in swaps:
         swapping.wait_recv()
     for own in range(2):
-        scores_of(2 * p + own)
-    for own in range(2):
         project_row(2 - 2 * p + own)
-    for own in range(2):
         scores_of(2 - 2 * p + own)
 
-    def soften(i, unit_y):
-        for at in range(0, 16, ROWS):
-            part = sc[unit_y, i, 16 * at : 16 * (at + ROWS), :]
-            part = part + bf[at : at + ROWS].reshape(16 * ROWS, 512)
+    def soften(unit_y, i):
+        for unit_x in range(4):
+            rows = slice(64 * unit_x, 64 * unit_x + 64)
+            if i == 0:
+                for core in range(2):
+                    tiles = bias[core, unit_y, unit_x].astype(F32) * log2e
+                    bf[4 * unit_x : 4 * unit_x + 4, core, :, 0:256] = tiles[:, 0:8]
+                    bf[4 * unit_x : 4 * unit_x + 4, core, :, 256:512] = tiles[:, 8:16]
+            part = sc[unit_y, i, rows, :] + bf[4 * unit_x : 4 * unit_x + 4].reshape(64, 512)
             exps = jnp.exp2(part - jnp.max(part, axis=1, keepdims=True))
-            wb[i, 16 * at : 16 * (at + ROWS), :] = exps.astype(BF16)
+            wb[i, rows, :] = exps.astype(BF16)
 
     def mix(i):
         out = dot(wb[i], ve[i])
@@ -506,25 +516,15 @@
 
     def block(step):
         unit_y = y ^ step ^ (step >> 1)
-
-        @pl.when(step == 0)
-        def _():
-            for d in (1, 3, 2):
-                unit_wait(1, y, x ^ d)
-
-        @pl.when(step > 0)
-        def _():
-            unit_wait(0, unit_y, x)
-            for d in (1, 3, 2):
-                unit_wait(0, unit_y, x ^ d)
-                unit_wait(1, unit_y, x ^ d)
-
-        for core in range(2):
-            tiles = bias[core, unit_y].reshape(16, 16, 256).astype(F32) * log2e
-            bf[:, core, :, 0:256] = tiles[:, 0:8]
-            bf[:, core, :, 256:512] = tiles[:, 8:16]
+        own_y = isinstance(step, int)
+        for near in (0, 1, 3, 2):
+            for part in range(2):
+                if not own_y:
+                    unit_wait(0, unit_y, x ^ near, part)
+                if near:
+                    unit_wait(1, unit_y, x ^ near, part)
         for i in range(4):
-            soften(i, unit_y)
+            soften(unit_y, i)
             if i > 0:
                 mix(i - 1)
         mix(3)
@@ -561,7 +561,8 @@
                 device_id_type=MESH,
             ).start()
 
-    loop(0, 4, block)
+    block(0)
+    loop(1, 4, block)
 
     def gated_sent():
         wait_bytes(gs.at[:, pl.ds(0, 15)], send4)
@@ -638,7 +639,7 @@
             dma, dma,
             dma((2,)), dma((2,)),
             dma((2,)),
-            dma((4,)), dma((2, 4, 4)),
+            dma((2,)), dma((2, 4, 4, 2)),
             dma, dma,
         ],
         compiler_params=pltpu.CompilerParams(

time: 65.1 us -> 64.2 us (0.986)
  Pallas kernels: 64.3 us -> 63.4 us
    pallas_call x1, Pallas kernels: 64.3 us -> 63.4 us  [local(): pl.pallas_call(kernel, out_shape=jax.ShapeDtypeStruct((64, 16, 128), BF16...]
where the time goes in v7:
time: 64.2 us; the launch traced here: 64.1 us
  Pallas kernels  63.4 us (99%)
  local copies, waits for them, and re-layouts  0.71 us (1%)
    pallas_call x1, Pallas kernels, local(): pl.pallas_call(kernel, out_shape=jax.ShapeDtypeStruct((64, 16, 128), BF16...  63.4 us

profile of v7, /device:TPU:3, one launch (start us, length us, event | category | flops | bytes accessed | tf_op | source)
XLA Modules:
  0.0 64.1 jit_solution(15442640463678467498)
XLA Ops:
  0.0 63.4 %shard_map.82 = bf16[64,16,128]{2,1,0:T(8,128)(2,1)S(1)} custom-call(bf16[64,16,128]{2,1,0:T(8,128)(2,1)} %pair_hbm.1, s32[512]{0:T(512)} %mask_hbm.1, s32[4,128]{1,0:T(4,128)} %bitcast.2, bf16[128,512]{1,0:T(8,128)(2,1)} %proj_hbm.1, bf16[128,128]{1,0:T(8,128)(2,1)} %gate_hbm.1, bf16[128,128]{1,0:T(8,128)(2,1)} %tout_hbm.1, bf16[128,512]{1,0:T(8,128)(2,1)} %qkvg_hbm.1, ...), custom_call_target="tpu_custom_call" | custom-call | tf_op jit(solution)/shard_map/pallas_call | solution.py:585
  63.4 0.7 %copy.10 = bf16[64,16,128]{2,1,0:T(8,128)(2,1)} copy(bf16[64,16,128]{2,1,0:T(8,128)(2,1)S(1)} %shard_map.82) | data formatting | bytes 524288

commit v8 on v7

--- a/solution.py
+++ b/solution.py
@@ -51,7 +51,7 @@
     out_ref,
     pair_ref, mask_smem, mask_ref, proj_ref, gate_ref, tout_ref, qkvg_ref, abias_ref, aout_ref, loads,
     pr_buf, xn, nk, wpt, ms, sb, pt, gt, gate_t, tout_t, qkvg_t,
-    a_buf, lt, tr, s_buf, t_buf, tf, updt, n2t, bscr, bm, up,
+    a_buf, lt, tr, s_buf, t_buf, tf, updt, n2t, bscr, mask_wide, bm, up,
     x_buf, bias, kt, ve, qe, gq, bf, sc, wb, mixed, gs, h_buf,
     send1, recv1, fsend, frecv, send2, recv2, gsend, grecv, psend, precv, xsend, xrecv,
     bsend, bz, bu, send4, recv4,
@@ -114,7 +114,8 @@
         part = xn[pl.ds(k, 64, stride=16), :].astype(BF16)
         nk[k] = jnp.concatenate([part, part], axis=0)
 
-    two = mask_ref[pl.ds(r >> 1, 1), :].astype(F32)
+    mask_wide[0:4, :] = mask_ref[...]
+    two = mask_wide[pl.ds(r >> 1, 1), :].astype(F32)
     odd = (r & 1) == 1
     turned = swap(jnp.broadcast_to(two, (8, 128)))[0:1]
     is_left = (lane >> 6) == jnp.where(odd, 0, 1)
@@ -348,15 +349,15 @@
         norm_two = norm_over(updated, 0)
         n2t[s] = norm_two
         heads = dot(abias_ref[...], norm_two.astype(BF16))[0:4]
-        live = mask_ref[pl.ds(s & 3, 1), :] > 0
+        live = mask_wide[pl.ds(s & 3, 1), :] > 0
         bscr[s & 1, pl.ds(8 * ((s & 3) >> 1) + (s >> 2), 4, stride=2), :] = jnp.where(
             live, heads, -1000000000.0
         )
 
     loop(0, 8, home, unroll=8)
 
-    bm[:, 0:128] = bscr[0].astype(BF16)
-    bm[:, 128:256] = bscr[1].astype(BF16)
+    bm[:, 0:128] = bscr[0, 0:16, :].astype(BF16)
+    bm[:, 128:256] = bscr[1, 0:16, :].astype(BF16)
 
     def bias_copy(src, dst, sem, recv, row, col):
         return pltpu.make_async_remote_copy(
@@ -617,7 +618,8 @@
             pltpu.VMEM((2048, 128), F32),
             pltpu.VMEM((8, 128, 128), F32),
             pltpu.VMEM((8, 128, 128), F32),
-            pltpu.VMEM((2, 16, 128), F32),
+            pltpu.VMEM((2, 24, 128), F32),
+            pltpu.VMEM((16, 128), jnp.int32),
             pltpu.VMEM((16, 256), BF16),
             pltpu.VMEM((4, 512, 128), F32),
             pltpu.VMEM((4, 512, 128), BF16),

time: 64.2 us -> 64.2 us (level)
  no operation moved by 1% of the time
where the time goes in v8:
time: 64.2 us; the launch traced here: 64.1 us
  Pallas kernels  63.4 us (99%)
  local copies, waits for them, and re-layouts  0.71 us (1%)
    pallas_call x1, Pallas kernels, local(): pl.pallas_call(kernel, out_shape=jax.ShapeDtypeStruct((64, 16, 128), BF16...  63.4 us

profile of v8, /device:TPU:3, one launch (start us, length us, event | category | flops | bytes accessed | tf_op | source)
XLA Modules:
  0.0 64.1 jit_solution(3057945497055587065)
XLA Ops:
  0.0 63.4 %shard_map.82 = bf16[64,16,128]{2,1,0:T(8,128)(2,1)S(1)} custom-call(bf16[64,16,128]{2,1,0:T(8,128)(2,1)} %pair_hbm.1, s32[512]{0:T(512)} %mask_hbm.1, s32[4,128]{1,0:T(4,128)} %bitcast.2, bf16[128,512]{1,0:T(8,128)(2,1)} %proj_hbm.1, bf16[128,128]{1,0:T(8,128)(2,1)} %gate_hbm.1, bf16[128,128]{1,0:T(8,128)(2,1)} %tout_hbm.1, bf16[128,512]{1,0:T(8,128)(2,1)} %qkvg_hbm.1, ...), custom_call_target="tpu_custom_call" | custom-call | tf_op jit(solution)/shard_map/pallas_call | solution.py:586
  63.4 0.7 %copy.10 = bf16[64,16,128]{2,1,0:T(8,128)(2,1)} copy(bf16[64,16,128]{2,1,0:T(8,128)(2,1)S(1)} %shard_map.82) | data formatting | bytes 524288

commit v9 on v8

--- a/solution.py
+++ b/solution.py
@@ -427,7 +427,7 @@
     def straight(own):
         part = (zh >> 1) ^ own
         wait_bytes(bias.at[:, 0, 0, pl.ds(0, 2)], bz.at[part])
-        for d in (1, 3, 2):
+        for d in (2, 1, 3):
             for core in range(2):
                 unit_copy(core, y, x, part, 0, d).start()
                 unit_copy(core, y, x, part, d, 0).start()
@@ -436,12 +436,11 @@
         part = (zh >> 1) ^ own
         for near in (1, 3, 2):
             unit_wait(0, y, x ^ near, part)
-        for dy in (1, 3, 2):
-            for near in (1, 3, 2):
+            for dy in (2, 1, 3):
                 unit_copy(0, y, x ^ near, part, dy, 0).start()
-            unit_wait(1, y ^ dy, x, part)
-            for dx in (1, 3, 2):
-                unit_copy(1, y ^ dy, x, part, 0, dx).start()
+            unit_wait(1, y ^ near, x, part)
+            for dx in (2, 1, 3):
+                unit_copy(1, y ^ near, x, part, 0, dx).start()
 
     row_at = lax.broadcasted_iota(jnp.int32, (256, 64), 0)
     spread = ((row_at // 8) * 2 + row_at % 2 == lax.broadcasted_iota(jnp.int32, (256, 64), 1)).astype(

time: 64.2 us -> 64 us (level)
  no operation moved by 1% of the time
where the time goes in v9:
time: 64 us; the launch traced here: 63.9 us
  Pallas kernels  63.2 us (99%)
  local copies, waits for them, and re-layouts  0.71 us (1%)
    pallas_call x1, Pallas kernels, local(): pl.pallas_call(kernel, out_shape=jax.ShapeDtypeStruct((64, 16, 128), BF16...  63.2 us

profile of v9, /device:TPU:3, one launch (start us, length us, event | category | flops | bytes accessed | tf_op | source)
XLA Modules:
  0.0 63.9 jit_solution(10649087133972672865)
XLA Ops:
  0.0 63.2 %shard_map.82 = bf16[64,16,128]{2,1,0:T(8,128)(2,1)S(1)} custom-call(bf16[64,16,128]{2,1,0:T(8,128)(2,1)} %pair_hbm.1, s32[512]{0:T(512)} %mask_hbm.1, s32[4,128]{1,0:T(4,128)} %bitcast.2, bf16[128,512]{1,0:T(8,128)(2,1)} %proj_hbm.1, bf16[128,128]{1,0:T(8,128)(2,1)} %gate_hbm.1, bf16[128,128]{1,0:T(8,128)(2,1)} %tout_hbm.1, bf16[128,512]{1,0:T(8,128)(2,1)} %qkvg_hbm.1, ...), custom_call_target="tpu_custom_call" | custom-call | tf_op jit(solution)/shard_map/pallas_call | solution.py:585
  63.2 0.7 %copy.10 = bf16[64,16,128]{2,1,0:T(8,128)(2,1)} copy(bf16[64,16,128]{2,1,0:T(8,128)(2,1)S(1)} %shard_map.82) | data formatting | bytes 524288

commit v10 on v9

--- a/solution.py
+++ b/solution.py
@@ -77,7 +77,7 @@
             ]
         )
     ]
-    for fetch in fetches:
+    for fetch in fetches[:4]:
         fetch.start()
 
     barrier = pltpu.get_barrier_semaphore()
@@ -95,6 +95,9 @@
     for dz in range(4):
         greet(r ^ 4, c ^ (2 * dz + 1))
 
+    for fetch in fetches[4:]:
+        fetch.start()
+
     lane = lax.broadcasted_iota(jnp.int32, (1, 128), 1)
     low = lane < 64
 
@@ -104,7 +107,7 @@
     def swap(values):
         return pltpu.roll(values, 64, 1)
 
-    for fetch in fetches:
+    for fetch in fetches[:4]:
         fetch.wait()
 
     flat = pair_ref[...].astype(F32).reshape(1024, 128)
@@ -196,6 +199,8 @@
     pltpu.make_async_copy(pair_ref.at[pl.ds(2 * c, 2)], pr_buf.at[:, c], precv).start()
     sent.append(lambda: wait_bytes(pr_buf.at[:, pl.ds(0, 31)], psend))
 
+    for fetch in fetches[4:]:
+        fetch.wait()
     gate_t[...] = flip(gate_ref[...])
     tout_t[...] = flip(tout_ref[...])
     qkvg_t[...] = flip(qkvg_ref[...])

time: 64 us -> 63.5 us (level)
  no operation moved by 1% of the time
where the time goes in v10:
time: 63.5 us; the launch traced here: 63.4 us
  Pallas kernels  62.7 us (99%)
  local copies, waits for them, and re-layouts  0.71 us (1%)
    pallas_call x1, Pallas kernels, local(): pl.pallas_call(kernel, out_shape=jax.ShapeDtypeStruct((64, 16, 128), BF16...  62.7 us

profile of v10, /device:TPU:3, one launch (start us, length us, event | category | flops | bytes accessed | tf_op | source)
XLA Modules:
  0.0 63.4 jit_solution(10079003081684767032)
XLA Ops:
  0.0 62.7 %shard_map.82 = bf16[64,16,128]{2,1,0:T(8,128)(2,1)S(1)} custom-call(bf16[64,16,128]{2,1,0:T(8,128)(2,1)} %pair_hbm.1, s32[512]{0:T(512)} %mask_hbm.1, s32[4,128]{1,0:T(4,128)} %bitcast.2, bf16[128,512]{1,0:T(8,128)(2,1)} %proj_hbm.1, bf16[128,128]{1,0:T(8,128)(2,1)} %gate_hbm.1, bf16[128,128]{1,0:T(8,128)(2,1)} %tout_hbm.1, bf16[128,512]{1,0:T(8,128)(2,1)} %qkvg_hbm.1, ...), custom_call_target="tpu_custom_call" | custom-call | tf_op jit(solution)/shard_map/pallas_call | solution.py:590
  62.7 0.7 %copy.10 = bf16[64,16,128]{2,1,0:T(8,128)(2,1)} copy(bf16[64,16,128]{2,1,0:T(8,128)(2,1)S(1)} %shard_map.82) | data formatting | bytes 524288
